TPU v7x, 512 devices: a whole 4x4x16 slice. The times are simulated.
512 devices in a mesh: py: 32 (over x_hi, z), pz: 16 (over y, x_lo, core).
Axes of the slice: x: 4 (x_hi: 2, x_lo: 2; x = x_hi * 2 + x_lo), y: 4, z: 16, core: 2. Of those that a mesh axis runs over, the one named last changes fastest.
Arguments:
- state: bfloat16 [64, 192, 4096], P(None, 'py', 'pz'), may hold values from -6 to 6
- cotangent: bfloat16 [64, 192, 4096], P(None, 'py', 'pz'), may hold values from -6 to 6
- spectral_y: bfloat16 [2, 32, 4096], replicated, may hold values from -0.5 to 0.5
- spectral_z: bfloat16 [2, 32, 4096], replicated, may hold values from -0.5 to 0.5
- w_in: bfloat16 [64, 256], replicated, may hold values from -0.75 to 0.75
- w_out: bfloat16 [256, 64], replicated, may hold values from -0.375 to 0.375
Outputs:
- grad_state: bfloat16 [64, 192, 4096], P(None, 'py', 'pz')
- grad_spectral_y: bfloat16 [2, 32, 4096], replicated
- grad_spectral_z: bfloat16 [2, 32, 4096], replicated
- grad_w_in: bfloat16 [64, 256], replicated
- grad_w_out: bfloat16 [256, 64], replicated
All inputs are finite; a program needn't handle non-finite values.
Results may differ from a plain program's by a relative error of at most 0.0076.
Values may be sent and summed in bfloat16 or wider, within the bound.
A program may use at most 64 MiB of HBM per device.

v0:
```python
import math

import jax
import jax.numpy as jnp
from jax import lax
from jax.sharding import PartitionSpec as P

MODES = 32
LEN_Y = 192
LEN_Z = 128
XCELLS = 32


HIGHEST = lax.Precision.HIGHEST


def dft_tables(length, mode_count):
    positions = jnp.arange(length, dtype=jnp.int32)
    frequency = jnp.arange(mode_count, dtype=jnp.int32)
    phase_angle = (jnp.outer(positions, frequency) % length).astype(jnp.float32) * (
        2.0 * math.pi / length
    )
    cosine_table = jnp.cos(phase_angle)
    sine_table = jnp.sin(phase_angle)
    weighting = jnp.where(frequency == 0, 1.0, 2.0).astype(jnp.float32) / length
    inverse_re = (cosine_table * weighting[None, :]).T
    inverse_im = -(sine_table * weighting[None, :]).T
    return (cosine_table, -sine_table, inverse_re, inverse_im)


def contract_form(form, first_arg, second_arg):
    return jnp.einsum(form, first_arg, second_arg, precision=HIGHEST)


def dense_product(first_arg, second_arg):
    return jnp.dot(first_arg, second_arg, precision=HIGHEST)


def pair_product(first_arg, second_arg):
    return lax.dot_general(
        first_arg, second_arg, (((1,), (1,)), ((), ())), preferred_element_type=jnp.float32
    )


def spectra(lines, tables, channel_count):
    length, spread, merged = lines.shape
    flat = lines.astype(jnp.float32).reshape(length, spread * merged)
    shape_out = (tables[0].shape[1], spread, channel_count, merged // channel_count)
    spec_re = dense_product(tables[0].T, flat).reshape(shape_out)
    spec_im = dense_product(tables[1].T, flat).reshape(shape_out)
    return (spec_re, spec_im)


def branch_forward(lines, weights, tables, channel_count):
    length, spread, merged = lines.shape
    spec_re, spec_im = spectra(lines, tables, channel_count)
    weight_re = weights[0]
    weight_im = weights[1]
    mix_form = "kacb,kco->kaob"
    mixed_re = contract_form(mix_form, spec_re, weight_re) - contract_form(
        mix_form, spec_im, weight_im
    )
    mixed_im = contract_form(mix_form, spec_im, weight_re) + contract_form(
        mix_form, spec_re, weight_im
    )
    mode_count = mixed_re.shape[0]
    result = dense_product(tables[2].T, mixed_re.reshape(mode_count, -1)) + dense_product(
        tables[3].T, mixed_im.reshape(mode_count, -1)
    )
    return (result.reshape(length, spread, merged), spec_re, spec_im)


def branch_backward(lines, spec_re, spec_im, weights, tables):
    length, spread, merged = lines.shape
    forward_re, forward_im, inverse_re, inverse_im = tables
    flat = lines.astype(jnp.float32).reshape(length, spread * merged)
    grad_re = dense_product(inverse_re, flat).reshape(spec_re.shape)
    grad_im = dense_product(inverse_im, flat).reshape(spec_re.shape)
    weight_re = weights[0]
    weight_im = weights[1]
    adjoint_form = "kaob,kco->kacb"
    outer_form = "kacb,kaob->kco"
    spec_grad_re = contract_form(adjoint_form, grad_re, weight_re) + contract_form(
        adjoint_form, grad_im, weight_im
    )
    spec_grad_im = contract_form(adjoint_form, grad_im, weight_re) - contract_form(
        adjoint_form, grad_re, weight_im
    )
    delta_re = contract_form(outer_form, spec_re, grad_re) + contract_form(
        outer_form, spec_im, grad_im
    )
    delta_im = contract_form(outer_form, spec_re, grad_im) - contract_form(
        outer_form, spec_im, grad_re
    )
    mode_count = spec_re.shape[0]
    field_grad = dense_product(forward_re, spec_grad_re.reshape(mode_count, -1)) + dense_product(
        forward_im, spec_grad_im.reshape(mode_count, -1)
    )
    return (field_grad.reshape(length, spread, merged), jnp.stack([delta_re, delta_im]))


def y_layout(block):
    channel_count, rows_local, depth_local, column_count = block.shape
    return jnp.transpose(block, (1, 3, 0, 2)).reshape(
        rows_local, column_count, channel_count * depth_local
    )


def z_layout(block):
    channel_count, rows_local, depth_local, column_count = block.shape
    return jnp.transpose(block, (2, 3, 0, 1)).reshape(
        depth_local, column_count, channel_count * rows_local
    )


def from_y_layout(lines, channel_count):
    rows_local, column_count, merged = lines.shape
    return jnp.transpose(
        lines.reshape(rows_local, column_count, channel_count, merged // channel_count),
        (2, 0, 3, 1),
    )


def from_z_layout(lines, channel_count):
    depth_local, column_count, merged = lines.shape
    return jnp.transpose(
        lines.reshape(depth_local, column_count, channel_count, merged // channel_count),
        (2, 3, 0, 1),
    )


def on_device(state, cotangent, spectral_y, spectral_z, w_in, w_out):
    channel_count, rows_local, merged_cells = state.shape
    depth_local = LEN_Z // lax.axis_size("pz")
    column_count = merged_cells // depth_local
    field_block = state.reshape(channel_count, rows_local, depth_local, column_count)
    cot_field = cotangent.reshape(channel_count, rows_local, depth_local, column_count)
    weights_y = spectral_y.astype(jnp.float32).reshape(2, MODES, channel_count, channel_count)
    weights_z = spectral_z.astype(jnp.float32).reshape(2, MODES, channel_count, channel_count)
    tables_y = dft_tables(LEN_Y, MODES)
    tables_z = dft_tables(LEN_Z, MODES)
    field_y = y_layout(field_block)
    field_z = z_layout(field_block)
    lines_y = lax.all_to_all(field_y, "py", split_axis=1, concat_axis=0, tiled=True)
    lines_z = lax.all_to_all(field_z, "pz", split_axis=1, concat_axis=0, tiled=True)
    result_y, real_y, imag_y = branch_forward(lines_y, weights_y, tables_y, channel_count)
    result_z, real_z, imag_z = branch_forward(lines_z, weights_z, tables_z, channel_count)
    branch_y = lax.all_to_all(
        result_y.astype(jnp.bfloat16), "py", split_axis=0, concat_axis=1, tiled=True
    )
    branch_z = lax.all_to_all(
        result_z.astype(jnp.bfloat16), "pz", split_axis=0, concat_axis=1, tiled=True
    )
    branch_y = from_y_layout(branch_y, channel_count)
    branch_z = from_z_layout(branch_z, channel_count)
    mixed_sum = (branch_y.astype(jnp.float32) + branch_z.astype(jnp.float32)).astype(jnp.bfloat16)
    flattened = mixed_sum.reshape(channel_count, -1)
    pre_act = jnp.dot(w_in.T, flattened, preferred_element_type=jnp.float32)
    activated, pullback = jax.vjp(jax.nn.gelu, pre_act)
    activated = activated.astype(jnp.bfloat16)
    cot_flat = cot_field.reshape(channel_count, -1)
    grad_act = jnp.dot(w_out, cot_flat, preferred_element_type=jnp.float32)
    grad_pre = pullback(grad_act)[0].astype(jnp.bfloat16)
    mlp_parts = (pair_product(flattened, grad_pre), pair_product(activated, cot_flat))
    grad_mixed = jnp.dot(w_in, grad_pre, preferred_element_type=jnp.float32).astype(jnp.bfloat16)
    grad_mixed = grad_mixed.reshape(channel_count, rows_local, depth_local, column_count)
    grad_y = y_layout(grad_mixed)
    grad_z = z_layout(grad_mixed)
    cot_lines_y = lax.all_to_all(grad_y, "py", split_axis=1, concat_axis=0, tiled=True)
    cot_lines_z = lax.all_to_all(grad_z, "pz", split_axis=1, concat_axis=0, tiled=True)
    local_back_y, y_parts = branch_backward(cot_lines_y, real_y, imag_y, weights_y, tables_y)
    back_y = lax.all_to_all(
        local_back_y.astype(jnp.bfloat16), "py", split_axis=0, concat_axis=1, tiled=True
    )
    local_back_z, z_parts = branch_backward(cot_lines_z, real_z, imag_z, weights_z, tables_z)
    back_z = lax.all_to_all(
        local_back_z.astype(jnp.bfloat16), "pz", split_axis=0, concat_axis=1, tiled=True
    )
    sum_in, sum_out, y_parts, z_parts = lax.psum(
        (mlp_parts[0], mlp_parts[1], y_parts, z_parts), ("py", "pz")
    )
    mlp_parts = (sum_in, sum_out)
    back_y = from_y_layout(back_y, channel_count)
    back_z = from_z_layout(back_z, channel_count)
    summed_grad = (
        cot_field.astype(jnp.float32) + back_y.astype(jnp.float32) + back_z.astype(jnp.float32)
    ).astype(jnp.bfloat16)
    grad_state = summed_grad.reshape(channel_count, rows_local, merged_cells)
    scale_y = 1.0 / math.sqrt(XCELLS * LEN_Z)
    scale_z = 1.0 / math.sqrt(XCELLS * LEN_Y)
    scale_mlp = 1.0 / math.sqrt(XCELLS * LEN_Y * LEN_Z)
    grad_spectral_y = (
        (y_parts * scale_y).astype(jnp.bfloat16).reshape(2, MODES, channel_count * channel_count)
    )
    grad_spectral_z = (
        (z_parts * scale_z).astype(jnp.bfloat16).reshape(2, MODES, channel_count * channel_count)
    )
    grad_w_in = (mlp_parts[0] * scale_mlp).astype(jnp.bfloat16)
    grad_w_out = (mlp_parts[1] * scale_mlp).astype(jnp.bfloat16)
    return (grad_state, grad_spectral_y, grad_spectral_z, grad_w_in, grad_w_out)


def solution(mesh):
    in_specs = (P(None, "py", "pz"), P(None, "py", "pz"), P(), P(), P(), P())
    out_specs = (P(None, "py", "pz"), P(), P(), P(), P())
    return jax.shard_map(
        on_device, mesh=mesh, in_specs=in_specs, out_specs=out_specs, check_vma=False
    )
```

profile of v0, /device:TPU:1, one launch (start us, length us, event | category | flops | bytes accessed | tf_op | source)
XLA Modules:
  0.0 730.0 jit_solution(9501466872975114673)
XLA Ops:
  10.2 10.2 %all-to-all-start.2 = ((bf16[8,32,384]{2,0,1:T(8,128)(2,1)}), bf16[8,32,384]{2,0,1:T(8,128)(2,1)S(1)}, u32[]{:S(2)}, u32[]{:S(2)}) async-start(bf16[8,32,384]{2,0,1:T(8,128)(2,1)} %copy.206), calls=%async_computation.2 | async-start | bytes 393216 | tf_op jit(solution)/shard_map/all_to_all | solution.py:145
  24.3 2.8 all-to-all-done.2
  27.1 14.2 %all-to-all-start = ((bf16[6,32,512]{2,0,1:T(8,128)(2,1)}), bf16[6,32,512]{2,0,1:T(8,128)(2,1)}, u32[]{:S(2)}, u32[]{:S(2)}) async-start(bf16[6,32,512]{2,0,1:T(8,128)(2,1)} %copy.193), calls=%async_computation | async-start | bytes 524288 | tf_op jit(solution)/shard_map/all_to_all | solution.py:144
  52.9 9.6 %all-to-all-done = bf16[6,32,512]{2,0,1:T(8,128)(2,1)} async-done(((bf16[6,32,512]{2,0,1:T(8,128)(2,1)}), bf16[6,32,512]{2,0,1:T(8,128)(2,1)}, u32[]{:S(2)}, u32[]{:S(2)}) %all-to-all-start) | async-done | bytes 196640 | tf_op jit(solution)/shard_map/all_to_all | solution.py:144
  62.5 7.8 %all-to-all-start.3 = ((bf16[128,2,384]{2,1,0:T(2,128)(2,1)}), bf16[128,2,384]{2,1,0:T(2,128)(2,1)}, u32[]{:S(2)}, u32[]{:S(2)}) async-start(bf16[128,2,384]{2,1,0:T(2,128)(2,1)} %convert_element_type.176), calls=%async_computation.3 | async-start | bytes 393216 | tf_op jit(solution)/shard_map/all_to_all | solution.py:151
  80.0 4.6 all-to-all-start.1
  87.2 10.0 %reshape.248 = f32[8,32,64,6]{3,2,0,1:T(8,128)} reshape(f32[8,16,2,384]{3,0,2,1:T(8,128)S(1)} %copy.217) | data formatting | bytes 786432 | tf_op jit(solution)/shard_map/convert_element_type | solution.py:156
  97.2 8.0 %copy.218 = f32[8,32,64,6]{1,0,2,3:T(8,128)} copy(f32[8,32,64,6]{3,2,0,1:T(8,128)} %reshape.248) | data formatting | bytes 786432 | tf_op jit(solution)/shard_map/convert_element_type | solution.py:156
  108.8 2.9 fusion.8
  120.7 2.4 copy.237
  123.0 6.9 all-to-all-start.6
  131.2 2.3 copy.223
  133.5 2.1 fusion.255
  136.7 22.6 %all-to-all-start.4 = ((bf16[6,32,512]{2,0,1:T(8,128)(2,1)}), bf16[6,32,512]{2,0,1:T(8,128)(2,1)}, u32[]{:S(2)}, u32[]{:S(2)}) async-start(bf16[6,32,512]{2,0,1:T(8,128)(2,1)} %copy.223), calls=%async_computation.4 | async-start | bytes 524288 | tf_op jit(solution)/shard_map/all_to_all | solution.py:169
  173.7 1.9 fusion.12
  175.7 2.2 fusion.14
  179.4 5.1 all-to-all-start.7
  194.1 2.5 fusion.26
  200.5 2.7 fusion.10
  203.3 14.3 %all-to-all-start.5 = ((bf16[32,2,1536]{2,1,0:T(2,128)(2,1)}), bf16[32,2,1536]{2,1,0:T(2,128)(2,1)S(1)}, u32[]{:S(2)}, u32[]{:S(2)}) async-start(bf16[32,2,1536]{2,1,0:T(2,128)(2,1)} %reshape.273), calls=%async_computation.5 | async-start | bytes 393216 | tf_op jit(solution)/shard_map/all_to_all | solution.py:172
  224.1 10.1 %reshape.250 = f32[8,32,64,6]{3,2,0,1:T(8,128)} reshape(f32[8,16,2,384]{3,0,2,1:T(8,128)S(1)} %copy.248) | data formatting | bytes 786432 | tf_op jit(solution)/shard_map/convert_element_type | solution.py:186
  234.2 5.5 copy.249
  243.4 471.9 %all-reduce.3.cloned.1.call-done = (f32[2,32,64,64]{3,2,1,0:T(8,128)}, f32[2,32,64,64]{3,2,1,0:T(8,128)}, f32[64,256]{1,0:T(8,128)}, f32[256,64]{0,1:T(8,128)}) async-done(((f32[2,32,64,64]{3,2,1,0:T(8,128)}, f32[2,32,64,64]{3,2,1,0:T(8,128)}, f32[64,256]{1,0:T(8,128)}, f32[256,64]{0,1:T(8,128)}), (f32[2,32,64,64]{3,2,1,0:T(8,128)}, f32[2,32,64,64]{3,2,1,0:T(8,128)}, f32[64,256]{1,0:T(8,128)}, ...) | async-done | bytes 2228240 | tf_op jit(solution)/shard_map/psum | solution.py:179
  715.3 2.8 multiply_convert_fusion
  (145 shorter events, 89.4 us)
Async XLA Ops:
  7.2 106.1 %copy-start = (bf16[64,256]{1,0:T(8,128)(2,1)S(1)}, bf16[64,256]{1,0:T(8,128)(2,1)}, u32[]{:S(2)}) copy-start(bf16[64,256]{1,0:T(8,128)(2,1)} %param.10) | copy-start | bytes 98308
  9.0 13.0 %copy-start.10 = (bf16[2,32,4096]{2,1,0:T(8,128)(2,1)S(1)}, bf16[2,32,4096]{2,1,0:T(8,128)(2,1)}, u32[]{:S(2)}) copy-start(bf16[2,32,4096]{2,1,0:T(8,128)(2,1)} %param.8) | copy-start | bytes 1572868
  10.2 16.9 %all-to-all-start.2 = ((bf16[8,32,384]{2,0,1:T(8,128)(2,1)}), bf16[8,32,384]{2,0,1:T(8,128)(2,1)S(1)}, u32[]{:S(2)}, u32[]{:S(2)}) async-start(bf16[8,32,384]{2,0,1:T(8,128)(2,1)} %copy.206), calls=%async_computation.2 | async-start | bytes 393216 | tf_op jit(solution)/shard_map/all_to_all | solution.py:145
  22.0 1.1 copy-start.11
  27.1 35.4 %all-to-all-start = ((bf16[6,32,512]{2,0,1:T(8,128)(2,1)}), bf16[6,32,512]{2,0,1:T(8,128)(2,1)}, u32[]{:S(2)}, u32[]{:S(2)}) async-start(bf16[6,32,512]{2,0,1:T(8,128)(2,1)} %copy.193), calls=%async_computation | async-start | bytes 524288 | tf_op jit(solution)/shard_map/all_to_all | solution.py:144
  62.5 17.5 %all-to-all-start.3 = ((bf16[128,2,384]{2,1,0:T(2,128)(2,1)}), bf16[128,2,384]{2,1,0:T(2,128)(2,1)}, u32[]{:S(2)}, u32[]{:S(2)}) async-start(bf16[128,2,384]{2,1,0:T(2,128)(2,1)} %convert_element_type.176), calls=%async_computation.3 | async-start | bytes 393216 | tf_op jit(solution)/shard_map/all_to_all | solution.py:151
  72.0 2.3 copy-start.2
  80.0 25.2 %all-to-all-start.1 = ((bf16[32,2,1536]{2,1,0:T(2,128)(2,1)}), bf16[32,2,1536]{2,1,0:T(2,128)(2,1)}, u32[]{:S(2)}, u32[]{:S(2)}) async-start(bf16[32,2,1536]{2,1,0:T(2,128)(2,1)} %reshape.271), calls=%async_computation.1 | async-start | bytes 393216 | tf_op jit(solution)/shard_map/all_to_all | solution.py:148
  111.7 2.0 copy-start.12
  113.7 1.3 copy-start.15
  123.0 13.7 %all-to-all-start.6 = ((bf16[8,32,384]{2,0,1:T(8,128)(2,1)}), bf16[8,32,384]{2,0,1:T(8,128)(2,1)}, u32[]{:S(2)}, u32[]{:S(2)}) async-start(bf16[8,32,384]{2,0,1:T(8,128)(2,1)} %copy.237), calls=%async_computation.6 | async-start | bytes 393216 | tf_op jit(solution)/shard_map/all_to_all | solution.py:170
  136.7 42.7 %all-to-all-start.4 = ((bf16[6,32,512]{2,0,1:T(8,128)(2,1)}), bf16[6,32,512]{2,0,1:T(8,128)(2,1)}, u32[]{:S(2)}, u32[]{:S(2)}) async-start(bf16[6,32,512]{2,0,1:T(8,128)(2,1)} %copy.223), calls=%async_computation.4 | async-start | bytes 524288 | tf_op jit(solution)/shard_map/all_to_all | solution.py:169
  179.4 7.4 %copy-start.3 = (f32[32,64,8]{1,0,2:T(8,128)S(1)}, f32[32,64,8]{1,0,2:T(8,128)}, u32[]{:S(2)}) copy-start(f32[32,64,8]{1,0,2:T(8,128)} %copy-done.2) | copy-start | bytes 196612
  179.4 23.9 %all-to-all-start.7 = ((bf16[128,2,384]{2,1,0:T(2,128)(2,1)}), bf16[128,2,384]{2,1,0:T(2,128)(2,1)}, u32[]{:S(2)}, u32[]{:S(2)}) async-start(bf16[128,2,384]{2,1,0:T(2,128)(2,1)} %convert_element_type.194), calls=%async_computation.7 | async-start | bytes 393216 | tf_op jit(solution)/shard_map/all_to_all | solution.py:176
  186.2 6.8 copy-start.4
  186.8 1.8 copy-start.6
  191.4 2.7 copy-start.7
  199.7 18.1 %copy-start.5 = (f32[32,64,8]{1,0,2:T(8,128)S(1)}, f32[32,64,8]{1,0,2:T(8,128)}, u32[]{:S(2)}) copy-start(f32[32,64,8]{1,0,2:T(8,128)} %copy-done.4) | copy-start | bytes 196612
  203.3 36.4 %all-to-all-start.5 = ((bf16[32,2,1536]{2,1,0:T(2,128)(2,1)}), bf16[32,2,1536]{2,1,0:T(2,128)(2,1)S(1)}, u32[]{:S(2)}, u32[]{:S(2)}) async-start(bf16[32,2,1536]{2,1,0:T(2,128)(2,1)} %reshape.273), calls=%async_computation.5 | async-start | bytes 393216 | tf_op jit(solution)/shard_map/all_to_all | solution.py:172
  217.5 497.8 %all-reduce.3.cloned.1.call-start = ((), (), s32[]{:S(2)}) async-start(), calls=%async_computation.8 | async-start | bytes 8650752 | tf_op jit(solution)/shard_map/psum | solution.py:179
  221.3 0.9 copy-start.9
  718.2 4.5 copy-start.1
  718.2 3.2 copy-start.14
  718.2 3.9 copy-start.13
  (1 other events, 0.9 us)
Sparse Core Ops, SparseCore 0:
  224.1 491.2 all-reduce.2
where the time goes:
time: 739 us; the launch traced here: 730 us
  waiting for transfers between devices  485 us (66%)
  starting transfers between devices  86 us (12%)
  local copies, waits for them, and re-layouts  75.2 us (10%)
  matrix products  51.9 us (7%)
  other arithmetic  16.4 us (2%)
  between operations  15.2 us (2%)
    psum x1, waiting for transfers between devices, on_device(): lax.psum((mlp_parts[0], mlp_parts[1], y_parts, z_parts), ('py', 'pz'))  472 us
    dot_general x24, matrix products, contract_form(): return jnp.einsum(form, first_arg, second_arg, precision=HIGHEST)  33.9 us
    all_to_all x1, starting transfers between devices, on_device(): lax.all_to_all(grad_y, 'py', split_axis=1, concat_axis=0, tiled=True)  22.6 us
    convert_element_type x3, local copies, waits for them, and re-layouts, on_device(): branch_z.astype(jnp.float32)  18.1 us
    convert_element_type x3, local copies, waits for them, and re-layouts, on_device(): back_z.astype(jnp.float32)  15.6 us
  transfers between devices with their start and end apart: 9, of which 4 were waited for; matrix products, arithmetic and copies ran while one was open for 16% of the time, Pallas kernels for 0%

commit v1 on v0

v1 whole, which is shorter than its diff:
```python
import functools
import math

import jax
import jax.numpy as jnp
import numpy as np
from jax import lax
from jax.experimental import pallas as pl
from jax.experimental.pallas import tpu as pltpu
from jax.sharding import PartitionSpec as P

MESH = pl.DeviceIdType.MESH
BF, F32 = jnp.bfloat16, jnp.float32
CH, HID = 64, 256
YL, ZL = 6, 8
LANES = 128


def dot_nn(a, b):
    return lax.dot_general(a, b, (((1,), (0,)), ((), ())), preferred_element_type=F32)


def dot_nt(a, b):
    return lax.dot_general(a, b, (((1,), (1,)), ((), ())), preferred_element_type=F32)


def dot_tn(a, b):
    return lax.dot_general(a, b, (((0,), (0,)), ((), ())), preferred_element_type=F32)


def parts_of(value):
    high = value.astype(BF)
    return high, (value - high.astype(F32)).astype(BF)


def np_parts(table):
    high = table.astype(np.float32).astype(BF)
    low = (table - high.astype(np.float64)).astype(np.float32).astype(BF)
    return high, low


def base_tables(length, modes):
    phase = 2.0 * np.pi * (np.outer(np.arange(modes), np.arange(length)) % length) / length
    weight = np.where(np.arange(modes) == 0, 1.0, 2.0)[:, None] / length
    forward = (np.cos(phase), -np.sin(phase))
    inverse = (weight * np.cos(phase), -weight * np.sin(phase))
    return forward, inverse


def y_tables(pair, spans, modes):
    eye = np.eye(ZL)
    blocks = []
    for table in pair:
        cut = table.reshape(modes, spans, 3, 2)
        for odd in range(2):
            block = np.einsum("ksy,uv->kusyv", cut[..., odd], eye)
            blocks.append(block.reshape(modes * ZL, spans * 3 * ZL))
    return np.concatenate(blocks, 0)


def swap(value):
    return pltpu.roll(value, 64, 1)


def kernel(
    NP,
    NQ,
    xs, cs, my, mz, wi2, wo2, zfh, zfl, zah, zal, zfth, zftl, zath, zatl, ytab_hbm, ytabt_hbm,
    grad_out, mlp_out, spec_out,
    r1, c1, z1, y1s, y1, y2s, y2, z2s, z2, g1, z3, y3s, y3, y4s, y4, z4s, z4, o1,
    rss, rsr, ws, wr, wg, m1s, m1r, m2r,
    pre, gact, actb, gpb, mixb, uz, gz, vz,
    su, sg, dwy, ytab, ytabt, tab_sem, send_sem, recv_sem,
):
    modes = 2 * NQ
    rows = NP * 24
    vrows = modes * ZL
    p, q = lax.axis_index("py"), lax.axis_index("pz")

    barrier = pltpu.get_barrier_semaphore()

    @pl.loop(1, NP)
    def _(i):
        pl.semaphore_signal(barrier, inc=1, device_id=(lax.rem(p + i, NP), q), device_id_type=MESH)

    @pl.loop(1, NQ)
    def _(i):
        pl.semaphore_signal(barrier, inc=1, device_id=(p, lax.rem(q + i, NQ)), device_id_type=MESH)

    pl.semaphore_wait(barrier, NP - 1 + NQ - 1)

    lo = lax.broadcasted_iota(jnp.int32, (1, LANES), 1) < 64
    pending = []

    def send(kind, slot, source, landing, n):
        mine = p if kind == "py" else q

        @pl.loop(1, n)
        def _(i):
            t = lax.rem(mine + i, n)
            pltpu.make_async_remote_copy(
                src_ref=source(t),
                dst_ref=landing.at[mine],
                send_sem=send_sem.at[slot],
                recv_sem=recv_sem.at[slot],
                device_id=(t, q) if kind == "py" else (p, t),
                device_id_type=MESH,
            ).start()

        pending.append((kind, slot, landing, n))

    def drain(kind, slot, landing, n):
        span = landing.at[pl.ds(0, n - 1)]
        return pltpu.make_async_remote_copy(
            src_ref=span,
            dst_ref=span,
            send_sem=send_sem.at[slot],
            recv_sem=recv_sem.at[slot],
            device_id=(p, q),
            device_id_type=MESH,
        )

    def arrived(kind, slot, landing, n):
        drain(kind, slot, landing, n).wait_recv()

    def own(landing, at, value):
        landing[pl.ds(at, 1)] = value

    send("py", 0, lambda t: xs.at[t], r1, NP)
    own(r1, p, xs[pl.ds(p, 1)])
    copies = [
        pltpu.make_async_copy(ytab_hbm, ytab, tab_sem.at[0]),
        pltpu.make_async_copy(ytabt_hbm, ytabt, tab_sem.at[1]),
    ]
    for copy in copies:
        copy.start()
    uz[...] = jnp.zeros_like(uz)
    gz[...] = jnp.zeros_like(gz)
    for copy in copies:
        copy.wait()
    arrived("py", 0, r1, NP)

    def lines(block):
        return block.astype(F32).reshape(rows, LANES).astype(BF)

    def y_analysis(which, field):
        def part(j):
            at = pl.ds(j * vrows, vrows)
            return dot_nn(ytab[which, 0, at], field) + dot_nn(ytab[which, 1, at], field)

        spec = jnp.where(lo, part(0) + swap(part(1)), swap(part(2)) + part(3))
        return spec.astype(BF).reshape(NQ, 2 * ZL, LANES)

    def y_synthesis(which, spec):
        value = spec.astype(F32).reshape(vrows, LANES)
        other = swap(value)
        pieces = [
            jnp.where(lo, value, 0.0), jnp.where(lo, 0.0, other),
            jnp.where(lo, other, 0.0), jnp.where(lo, 0.0, value),
        ]
        stacked = jnp.concatenate(pieces, 0).astype(BF)
        return dot_nn(ytabt[which, 0], stacked) + dot_nn(ytabt[which, 1], stacked)

    def z_analysis(high, low, landing, store):
        both = jnp.concatenate([high[...], low[...]], 1)
        for h in range(2):
            block = landing[:, h].astype(F32)
            for j in range(3):
                cells = block[:, j * ZL:(j + 1) * ZL].reshape(NQ * ZL, LANES).astype(BF)
                spec = dot_nn(both, jnp.concatenate([cells, cells], 0))
                re, im = spec[:modes], spec[modes:]
                at = (h * 3 + j) * 2 * modes
                store[pl.ds(at, modes), :] = jnp.where(lo, re, swap(im))
                store[pl.ds(at + modes, modes), :] = jnp.where(lo, swap(re), im)

    def z_synthesis(high, low, source, sends):
        three = jnp.concatenate([high[...], high[...], low[...]], 1)
        for h in range(2):
            out = []
            for j in range(3):
                at = (h * 3 + j) * 2 * modes
                even, odd = source[pl.ds(at, modes), :], source[pl.ds(at + modes, modes), :]
                spec = jnp.concatenate(
                    [jnp.where(lo, even, swap(odd)), jnp.where(lo, swap(even), odd)], 0
                )
                sh, sl = parts_of(spec)
                cells = dot_nn(three, jnp.concatenate([sh, sl, sh], 0))
                out.append(cells.reshape(NQ, ZL, LANES))
            sends[:, h] = jnp.concatenate(out, 1).astype(BF)

    unroll = min(8, modes)

    def z_mix(source, store, transposed):
        @pl.loop(0, modes // unroll)
        def _(step):
            for j in range(unroll):
                k = step * unroll + j
                high, low = parts_of(source[pl.ds(k, 16, stride=modes), :])
                both = jnp.concatenate([high, low], 0)
                got = dot_nt(both, mz[k]) if transposed else dot_nn(both, mz[k])
                store[pl.ds(k, 16, stride=modes), :] = got[:16] + got[16:]

    def fold(outer):
        top, bottom = outer[:64], swap(outer[64:])
        return top + jnp.where(lo, bottom, -bottom)

    second = (lax.broadcasted_iota(jnp.int32, (vrows, 1), 0) // ZL) % 2 == 1

    def y_mix(landing, dot):
        value = landing[...].reshape(vrows, LANES)
        return jnp.where(second, dot(value, my[1]), dot(value, my[0])).astype(BF).reshape(
            NQ, 2 * ZL, LANES
        )

    send("pz", 1, lambda t: r1.at[pl.ds(2 * t, 2)], z1, NQ)
    send("py", 2, lambda t: cs.at[t], c1, NP)
    own(z1, q, r1[pl.ds(2 * q, 2)].reshape(1, 2, 24, LANES))
    own(c1, p, cs[pl.ds(p, 1)])
    y1s[...] = y_analysis(0, lines(r1[...]))
    send("pz", 3, lambda t: y1s.at[t], y1, NQ)
    own(y1, q, y1s[pl.ds(q, 1)])
    arrived("pz", 3, y1, NQ)
    y2s[...] = y_mix(y1, dot_nn)
    send("pz", 4, lambda t: y2s.at[t], y2, NQ)
    own(y2, q, y2s[pl.ds(q, 1)])
    arrived("pz", 1, z1, NQ)
    z_analysis(zfh, zfl, z1, uz)
    z_mix(uz, vz, False)
    z_synthesis(zath, zatl, vz, z2s)
    send("pz", 5, lambda t: z2s.at[t], z2, NQ)
    own(z2, q, z2s[pl.ds(q, 1)])
    arrived("pz", 4, y2, NQ)
    branch_y = y_synthesis(1, y2[...]).astype(BF)
    arrived("pz", 5, z2, NQ)
    branch_z = z2[...].astype(F32).reshape(rows, LANES)
    mixb[...] = (branch_y.astype(F32) + branch_z).astype(BF)

    pre[...] = dot_nn(mixb[...], wi2[...])
    arrived("py", 2, c1, NP)
    cot = lines(c1[...])
    gact[...] = dot_nn(cot, wo2[...])
    tile = 32 if rows % 32 == 0 else 16

    @pl.loop(0, rows // tile)
    def _(step):
        at = pl.ds(pl.multiple_of(step * tile, tile), tile)
        value = pre[at, :]
        root = math.sqrt(2.0 / math.pi)
        square = value * value
        bend = jnp.tanh(value * (root + (root * 0.044715) * square))
        half = 0.5 + 0.5 * bend
        slope = half + (0.5 * value) * (1.0 - bend * bend) * (root + (3.0 * root * 0.044715) * square)
        actb[at, :] = (value * half).astype(BF)
        gpb[at, :] = (gact[at, :] * slope).astype(BF)

    g1[...] = dot_nt(gpb[...], wi2[...]).reshape(NP, 24, LANES).astype(BF)

    send("pz", 6, lambda t: g1.at[pl.ds(2 * t, 2)], z3, NQ)
    own(z3, q, g1[pl.ds(2 * q, 2)].reshape(1, 2, 24, LANES))
    y3s[...] = y_analysis(1, lines(g1[...]))
    send("pz", 7, lambda t: y3s.at[t], y3, NQ)
    own(y3, q, y3s[pl.ds(q, 1)])

    def diagonal(both):
        return both[:64, :HID] + both[64:, HID:]

    dwi = diagonal(dot_tn(mixb[...], gpb[...]))
    dwo = diagonal(dot_tn(cot, actb[...]))
    share = 256 // NP
    m1s[...] = jnp.concatenate(
        [dwi[:, :LANES], dwi[:, LANES:], dwo[:, :LANES], dwo[:, LANES:]], 0
    ).reshape(NP, share, LANES)
    send("py", 8, lambda t: m1s.at[t], m1r, NP)
    own(m1r, p, m1s[pl.ds(p, 1)])

    arrived("pz", 7, y3, NQ)
    y4s[...] = y_mix(y3, dot_nt)
    send("pz", 9, lambda t: y4s.at[t], y4, NQ)
    own(y4, q, y4s[pl.ds(q, 1)])
    arrived("pz", 6, z3, NQ)
    z_analysis(zah, zal, z3, gz)

    @pl.loop(0, modes // unroll)
    def _(step):
        for j in range(unroll):
            k = step * unroll + j
            uh, ul = parts_of(uz[pl.ds(k, 16, stride=modes), :])
            gh, gl = parts_of(gz[pl.ds(k, 16, stride=modes), :])
            outer = dot_tn(jnp.concatenate([uh, ul, uh], 0), jnp.concatenate([gh, gh, gl], 0))
            rss[step * (unroll // 2) + j // 2, pl.ds((j % 2) * 64, 64), :] = fold(outer).astype(BF)

    send("pz", 10, lambda t: rss.at[t], rsr, NQ)
    own(rsr, q, rss[pl.ds(q, 1)])
    for landing, store in ((y1, su), (y3, sg)):
        value = landing[...].astype(F32)
        for j in range(2):
            at = value[:, j * ZL:(j + 1) * ZL]
            store[j] = at.reshape(NQ * ZL, LANES).astype(BF)

    @pl.loop(0, 2)
    def _(j):
        dwy[j] = fold(dot_tn(su[j], sg[j]))

    z_mix(gz, vz, True)
    z_synthesis(zfth, zftl, vz, z4s)
    send("pz", 11, lambda t: z4s.at[t], z4, NQ)
    own(z4, q, z4s[pl.ds(q, 1)])

    arrived("pz", 9, y4, NQ)
    back_y = y_synthesis(0, y4[...]).astype(BF)
    arrived("pz", 11, z4, NQ)
    back_z = z4[...].astype(F32).reshape(rows, LANES)
    total = cot.astype(F32) + back_y.astype(F32) + back_z
    o1[...] = total.reshape(NP, 24, LANES).astype(BF)
    send("py", 12, lambda t: o1.at[t], grad_out, NP)
    own(grad_out, p, o1[pl.ds(p, 1)])

    arrived("pz", 10, rsr, NQ)
    dwz = jnp.sum(rsr[...].astype(F32), axis=0)
    ws[...] = jnp.concatenate([dwy[0], dwy[1], dwz], 0).reshape(NP, share, LANES)
    send("py", 13, lambda t: ws.at[t], wr, NP)
    own(wr, p, ws[pl.ds(p, 1)])
    arrived("py", 8, m1r, NP)
    own(m2r, q, jnp.sum(m1r[...], axis=0, keepdims=True))
    send("pz", 14, lambda t: m2r.at[q], m2r, NQ)
    arrived("pz", 14, m2r, NQ)
    scale_mlp = 1.0 / math.sqrt(NP * (YL * NP) * (ZL * NQ))
    own(mlp_out, p, jnp.sum(m2r[...], axis=0, keepdims=True) * scale_mlp)
    send("py", 15, lambda t: mlp_out.at[p], mlp_out, NP)
    arrived("py", 13, wr, NP)
    scale_y = 1.0 / math.sqrt(NP * ZL * NQ)
    scale_z = 1.0 / math.sqrt(NP * YL * NP)
    scale = jnp.where(p < NP // 2, scale_y, scale_z)
    own(wg, p, (jnp.sum(wr[...], axis=0, keepdims=True) * scale).astype(BF))
    send("py", 16, lambda t: wg.at[p], wg, NP)
    arrived("py", 16, wg, NP)
    own(spec_out, q, wg[...].reshape(1, NP, share, LANES))
    send("pz", 17, lambda t: wg, spec_out, NQ)
    arrived("py", 12, grad_out, NP)
    arrived("py", 15, mlp_out, NP)
    arrived("pz", 17, spec_out, NQ)
    for item in pending:
        drain(*item).wait_send()


def on_device(NP, NQ, state, cotangent, spectral_y, spectral_z, w_in, w_out):
    modes = 2 * NQ
    rows = NP * 24
    vrows = modes * ZL
    share = 256 // NP

    def to_blocks(field):
        cut = field.reshape(CH, 3, 2, ZL, NP)
        return jnp.transpose(cut, (4, 1, 3, 2, 0)).reshape(NP, 24, LANES)

    def mixing(weights):
        re, im = weights[0], weights[1]
        return jnp.concatenate(
            [jnp.concatenate([re, im], -1), jnp.concatenate([-im, re], -1)], -2
        )

    own_y = lax.dynamic_slice_in_dim(spectral_y, 2 * lax.axis_index("pz"), 2, 1)
    my = mixing(own_y.reshape(2, 2, CH, CH))
    mz = mixing(spectral_z.reshape(2, modes, CH, CH))
    eye = jnp.eye(2, dtype=BF)
    wi2 = jnp.kron(eye, w_in)
    wo2 = jnp.kron(eye, w_out.T)

    forward_y, inverse_y = base_tables(YL * NP, modes)
    forward_z, inverse_z = base_tables(ZL * NQ, modes)
    tabs = [np_parts(y_tables(pair, NP, modes)) for pair in (forward_y, inverse_y)]
    ytab = jnp.asarray(np.stack([np.stack(t) for t in tabs]))
    ytabt = jnp.asarray(np.stack([np.stack([v.T for v in t]) for t in tabs]))
    zf = np_parts(np.concatenate(forward_z, 0))
    za = np_parts(np.concatenate(inverse_z, 0))
    small = [jnp.asarray(v) for v in (*zf, *za, zf[0].T, zf[1].T, za[0].T, za[1].T)]

    vmem = pl.BlockSpec(memory_space=pltpu.VMEM)
    hbm = pl.BlockSpec(memory_space=pl.ANY)
    V = pltpu.VMEM
    field = lambda: V((NP, 24, LANES), BF)
    zbuf = lambda: V((NQ, 2, 24, LANES), BF)
    ybuf = lambda: V((NQ, 2 * ZL, LANES), BF)
    scratch = [
        field(), field(), zbuf(), ybuf(), ybuf(), ybuf(), ybuf(), zbuf(), zbuf(),
        field(), zbuf(), ybuf(), ybuf(), ybuf(), ybuf(), zbuf(), zbuf(), field(),
        V((NQ, 2 * CH, LANES), BF), V((NQ, 2 * CH, LANES), BF),
        V((NP, share, LANES), F32), V((NP, share, LANES), F32), V((NP, share, LANES), BF),
        V((NP, share, LANES), F32), V((NP, share, LANES), F32), V((NQ, share, LANES), F32),
        V((rows, 2 * HID), F32), V((rows, 2 * HID), F32),
        V((rows, 2 * HID), BF), V((rows, 2 * HID), BF), V((rows, LANES), BF),
        V((16 * modes, LANES), F32), V((16 * modes, LANES), F32), V((16 * modes, LANES), F32),
        V((2, NQ * ZL, LANES), BF), V((2, NQ * ZL, LANES), BF), V((2, CH, LANES), F32),
        V((2, 2, 4 * vrows, rows), BF), V((2, 2, rows, 4 * vrows), BF),
        pltpu.SemaphoreType.DMA((2,)),
        pltpu.SemaphoreType.DMA((18,)),
        pltpu.SemaphoreType.DMA((18,)),
    ]
    grad, mlp, spec = pl.pallas_call(
        functools.partial(kernel, NP, NQ),
        out_shape=(
            jax.ShapeDtypeStruct((NP, 24, LANES), BF),
            jax.ShapeDtypeStruct((NP, share, LANES), F32),
            jax.ShapeDtypeStruct((NQ, NP, share, LANES), BF),
        ),
        in_specs=[vmem] * 14 + [hbm] * 2,
        out_specs=(vmem, vmem, vmem),
        scratch_shapes=scratch,
        compiler_params=pltpu.CompilerParams(
            collective_id=0, has_side_effects=True, vmem_limit_bytes=56 * 1024 * 1024
        ),
    )(to_blocks(state), to_blocks(cotangent), my, mz, wi2, wo2, *small, ytab, ytabt)

    grad_state = jnp.transpose(grad.reshape(NP, 3, ZL, 2, CH), (4, 1, 3, 2, 0)).reshape(state.shape)
    spec = spec.reshape(NQ, 2, 2, CH, 2, CH)
    spec = jnp.transpose(spec, (1, 4, 0, 2, 3, 5)).reshape(2, 2, modes, CH * CH)
    mlp = mlp.reshape(2, 2, CH, LANES).astype(BF)
    grad_w_in = jnp.transpose(mlp[0], (1, 0, 2)).reshape(CH, HID)
    grad_w_out = jnp.transpose(mlp[1], (0, 2, 1)).reshape(HID, CH)
    return (grad_state, spec[0], spec[1], grad_w_in, grad_w_out)


def solution(mesh):
    sizes = (mesh.shape["py"], mesh.shape["pz"])
    in_specs = (P(None, "py", "pz"), P(None, "py", "pz"), P(), P(), P(), P())
    out_specs = (P(None, "py", "pz"), P(), P(), P(), P())
    return jax.shard_map(
        functools.partial(on_device, *sizes),
        mesh=mesh,
        in_specs=in_specs,
        out_specs=out_specs,
        check_vma=False,
    )
```

time: 739 us -> 134 us (0.18); the launches traced: 730 us -> 133 us
  waiting for transfers between devices: 485 us -> 0 us
  Pallas kernels: 0 us -> 112 us
  starting transfers between devices: 86 us -> 0 us
  local copies, waits for them, and re-layouts: 75.2 us -> 16.6 us
  matrix products: 51.9 us -> 0 us
  between operations: 15.2 us -> 0.79 us
  other arithmetic: 16.4 us -> 4.45 us
    psum x1 -> x0, waiting for transfers between devices: 472 us -> none  [on_device(): lax.psum((mlp_parts[0], mlp_parts[1], y_parts, z_parts), ('py', 'pz'))]
    pallas_call x0 -> x1, Pallas kernels: none -> 112 us  [on_device(): pl.pallas_call(functools.partial(kernel, NP, NQ), out_shape=(jax.ShapeDty...]
    all_to_all x8 -> x0, starting transfers between devices: 85.7 us -> none  [the longest x1 22.6 us: on_device(): lax.all_to_all(grad_y, 'py', split_axis=1, concat_axis=0, tiled=True)]
    dot_general x45 -> x0, matrix products: 51.9 us -> none  [the longest x24 33.9 us: contract_form(): return jnp.einsum(form, first_arg, second_arg, precision=HIGHEST)]
    convert_element_type x14 -> x0, local copies, waits for them, and re-layouts: 41.9 us -> none  [the longest x3 18.1 us: on_device(): branch_z.astype(jnp.float32)]
    all_to_all x8 -> x0, waiting for transfers between devices: 13.4 us -> none  [the longest x1 9.57 us: on_device(): lax.all_to_all(field_y, 'py', split_axis=1, concat_axis=0, tiled=True)]
    convert_element_type x11 -> x2, other arithmetic: 13.3 us -> 1.01 us  [the longest x1 1 us: on_device(): mlp = mlp.reshape(2, 2, CH, LANES).astype(BF)]
    reshape x12 -> x6, local copies, waits for them, and re-layouts: 13.2 us -> 4.42 us  [the longest x2 1.76 us: to_blocks(): return jnp.transpose(cut, (4, 1, 3, 2, 0)).reshape(NP, 24, LANES)]
  transfers between devices with their start and end apart: 9 -> 0, of which waited for: 4 -> 0; matrix products, arithmetic and copies ran while one was open for 16% -> 0% of each run, Pallas kernels for 0% -> 0%
where the time goes in v1:
time: 134 us; the launch traced here: 133 us
  Pallas kernels  112 us (84%)
  local copies, waits for them, and re-layouts  16.6 us (12%)
  other arithmetic  4.45 us (3%)
    pallas_call x1, Pallas kernels, on_device(): pl.pallas_call(functools.partial(kernel, NP, NQ), out_shape=(jax.ShapeDty...  112 us
    unnamed x11, local copies, waits for them, and re-layouts  3.56 us
    squeeze x2, local copies, waits for them, and re-layouts, on_device(): return (grad_state, spec[0], spec[1], grad_w_in, grad_w_out)  3.23 us

profile of v1, /device:TPU:1, one launch (start us, length us, event | category | flops | bytes accessed | tf_op | source)
XLA Modules:
  0.0 133.4 jit_solution(16814665417369178636)
XLA Ops:
  0.7 1.0 constant_dynamic-slice_fusion.1
  1.8 0.7 maximum_maximum_fusion.1.my
  2.6 1.0 broadcast_multiply_fusion
  3.6 0.7 copy.41
  4.3 0.7 copy.40
  4.9 1.1 copy.28
  6.1 0.4 copy.29
  6.5 0.9 reshape.78.xs
  7.6 0.4 copy.31
  8.0 0.9 reshape.80.cs
  8.9 0.5 squeeze.27
  9.6 0.5 squeeze.26
  10.2 1.5 %maximum_maximum_fusion.mz = bf16[32,128,128]{2,1,0:T(8,128)(2,1)} fusion(bf16[32,64,64]{2,1,0:T(8,128)(2,1)S(1)} %squeeze.26, bf16[32,64,64]{2,1,0:T(8,128)(2,1)S(1)} %neg.7, bf16[32,64,64]{2,1,0:T(8,128)(2,1)S(1)} %squeeze.27), kind=kLoop, calls=%fused_computation | loop fusion | flops 4194304 | bytes 1835008 | tf_op jit(solution)/shard_map/concatenate | solution.py:358
  11.7 111.6 %shard_map.191 = (bf16[32,24,128]{2,1,0:T(8,128)(2,1)}, f32[32,8,128]{2,1,0:T(8,128)}, bf16[16,32,8,128]{3,2,1,0:T(8,128)(2,1)}) custom-call(bf16[32,24,128]{2,1,0:T(8,128)(2,1)} %reshape.78.xs, bf16[32,24,128]{2,1,0:T(8,128)(2,1)} %reshape.80.cs, bf16[2,128,128]{2,1,0:T(8,128)(2,1)} %maximum_maximum_fusion.1.my, ...), custom_call_target="tpu_custom_call" | custom-call | tf_op jit(solution)/shard_map/pallas_call | solution.py:399
  123.3 1.0 convert_element_type.14
  124.3 0.6 copy_bitcast_fusion
  125.0 1.1 reshape.81
  126.2 0.8 copy.37
  127.0 0.8 reshape.83
  127.9 1.8 %fusion = (bf16[1,2,16,2,64,64]{5,1,4,3,0,2:T(2,128)(2,1)S(1)}, bf16[1,2,16,2,64,64]{5,1,4,3,0,2:T(2,128)(2,1)S(1)}) fusion(bf16[2,2,16,2,64,64]{5,1,4,3,0,2:T(2,128)(2,1)S(1)} %bitcast.35), kind=kLoop, calls=%fused_computation.9 | loop fusion | bytes 2097152 | tf_op jit(solution)/shard_map/slice | solution.py:420
  129.6 0.3 copy.34
  129.9 1.6 %squeeze.29 = bf16[2,32,4096]{2,1,0:T(8,128)(2,1)} reshape(bf16[1,2,16,2,64,64]{5,4,3,2,1,0:T(8,128)(2,1)S(1)} %copy.34) | data formatting | bytes 1048576 | tf_op jit(solution)/shard_map/squeeze | solution.py:420
  131.5 0.3 copy.33
  131.8 1.6 %squeeze.28 = bf16[2,32,4096]{2,1,0:T(8,128)(2,1)} reshape(bf16[1,2,16,2,64,64]{5,4,3,2,1,0:T(8,128)(2,1)S(1)} %copy.33) | data formatting | bytes 1048576 | tf_op jit(solution)/shard_map/squeeze | solution.py:420
  (15 shorter events, 0.7 us)
Async XLA Ops:
  0.6 6.8 %copy-start.2 = (bf16[64,6,256]{2,0,1:T(8,128)(2,1)S(1)}, bf16[64,6,256]{2,0,1:T(8,128)(2,1)}, u32[]{:S(2)}) copy-start(bf16[64,6,256]{2,0,1:T(8,128)(2,1)} %param.17) | copy-start | bytes 589828
  4.3 4.7 %copy-start.1 = (bf16[2,32,4096]{2,1,0:T(8,128)(2,1)S(1)}, bf16[2,32,4096]{2,1,0:T(8,128)(2,1)}, u32[]{:S(2)}) copy-start(bf16[2,32,4096]{2,1,0:T(8,128)(2,1)} %param.19) | copy-start | bytes 1572868
  123.3 3.7 %copy-start = (bf16[16,32,8,128]{3,2,1,0:T(8,128)(2,1)S(1)}, bf16[16,32,8,128]{3,2,1,0:T(8,128)(2,1)}, u32[]{:S(2)}) copy-start(bf16[16,32,8,128]{3,2,1,0:T(8,128)(2,1)} %get-tuple-element.9) | copy-start | bytes 3145732

commit v2 on v1

v2 whole, which is shorter than its diff:
```python
import functools
import math

import jax
import jax.numpy as jnp
import numpy as np
from jax import lax
from jax.experimental import pallas as pl
from jax.experimental.pallas import tpu as pltpu
from jax.sharding import PartitionSpec as P

MESH = pl.DeviceIdType.MESH
BF, F32 = jnp.bfloat16, jnp.float32
CH, HID = 64, 256
YL, ZL = 6, 8
LANES = 128


def dot_nn(a, b):
    return lax.dot_general(a, b, (((1,), (0,)), ((), ())), preferred_element_type=F32)


def dot_nt(a, b):
    return lax.dot_general(a, b, (((1,), (1,)), ((), ())), preferred_element_type=F32)


def dot_tn(a, b):
    return lax.dot_general(a, b, (((0,), (0,)), ((), ())), preferred_element_type=F32)


def parts_of(value):
    high = value.astype(BF)
    return high, (value - high.astype(F32)).astype(BF)


def np_parts(table):
    high = table.astype(np.float32).astype(BF)
    low = (table - high.astype(np.float64)).astype(np.float32).astype(BF)
    return high, low


def base_tables(length, modes):
    phase = 2.0 * np.pi * (np.outer(np.arange(modes), np.arange(length)) % length) / length
    weight = np.where(np.arange(modes) == 0, 1.0, 2.0)[:, None] / length
    forward = (np.cos(phase), -np.sin(phase))
    inverse = (weight * np.cos(phase), -weight * np.sin(phase))
    return forward, inverse


def y_tables(pair, spans, modes):
    cuts = [table.reshape(modes, spans * 3, 2) for table in pair]
    return np.concatenate([cut[..., odd] for cut in cuts for odd in range(2)], 0)


def swap(value):
    return pltpu.roll(value, 64, 1)


def kernel(
    NP,
    NQ,
    state, cotangent, spectral_y, spectral_z, w_in, w_out,
    yf, ya, yft, yat, zfh, zfl, zah, zal, zfth, zftl, zath, zatl,
    grad_state, grad_sy, grad_sz, grad_in, grad_out,
    xs, cs, r1, c1, z1, y1s, y1, y2s, y2, z2s, z2, g1, z3, y3s, y3, y4s, y4, z4s, z4, o1, f1,
    us, ur, gs, gr, ws, wr, wg, parts, gathered, m1s, m1r, m2r, m3r,
    wi2, wo2, my, mz, pre, gact, actb, gpb, mixb, uz, gz, vz, su, sg, dws,
    cells_f, spec_f, turn_f, big_f,
    send_sem, recv_sem, ring_sem,
):
    modes = 2 * NQ
    rows = NP * 24
    vrows = modes * ZL
    share = 256 // NP
    half = NP // 2
    p, q = lax.axis_index("py"), lax.axis_index("pz")
    sibling = q + 1 - 2 * lax.rem(q, 2)

    barrier = pltpu.get_barrier_semaphore()

    @pl.loop(1, NP)
    def _(i):
        pl.semaphore_signal(barrier, inc=1, device_id=(lax.rem(p + i, NP), q), device_id_type=MESH)

    @pl.loop(1, NQ)
    def _(i):
        pl.semaphore_signal(barrier, inc=1, device_id=(p, lax.rem(q + i, NQ)), device_id_type=MESH)

    lo = lax.broadcasted_iota(jnp.int32, (1, LANES), 1) < 64
    pending = []

    def send(kind, slot, source, landing, n, span=(0, half)):
        def start(t, mine, device):
            pltpu.make_async_remote_copy(
                src_ref=source(t),
                dst_ref=landing.at[mine],
                send_sem=send_sem.at[slot],
                recv_sem=recv_sem.at[slot],
                device_id=device,
                device_id_type=MESH,
            ).start()

        if kind == "pz":

            @pl.loop(1, n)
            def _(i):
                t = lax.rem(q + i, n)
                start(t, q, (p, t))

        else:

            @pl.loop(*span)
            def _(i):
                far = half // 2 + (1 - 2 * lax.rem(i, 2)) * ((i + 1) // 2)
                step = lax.rem(p + far + half, half)
                sides = (0, 1) if kind == "py" else (kind,)
                for side in sides:
                    t = step + (lax.rem(p // half + 1 + side, 2) if kind == "py" else side) * half

                    @pl.when(t != p)
                    def _():
                        start(t, p, (t, q))

            if span[1] < half or kind != "py":
                return

        pending.append((slot, landing, n))

    def drain(slot, landing, n):
        span = landing.at[pl.ds(0, n - 1)]
        return pltpu.make_async_remote_copy(
            src_ref=span,
            dst_ref=span,
            send_sem=send_sem.at[slot],
            recv_sem=recv_sem.at[slot],
            device_id=(p, q),
            device_id_type=MESH,
        )

    def arrived(slot, landing, n):
        drain(slot, landing, n).wait_recv()

    def own(landing, at, value):
        landing[pl.ds(at, 1)] = value

    def to_blocks(source, blocks):
        for j in range(3):
            turn_f[...] = jnp.concatenate([source[2 * j], source[2 * j + 1]], 0).astype(F32).T
            for x in range(NP):
                big_f[pl.ds(x * 24 + j * ZL, ZL), :] = turn_f[pl.ds(x, ZL, stride=NP), :]
        blocks[...] = big_f[:rows, :].reshape(NP, 24, LANES).astype(BF)

    def from_blocks(blocks, target):
        big_f[:rows, :] = blocks[...].astype(F32).reshape(rows, LANES)
        for j in range(3):
            cells = [big_f[pl.ds(j * ZL + z, NP, stride=24), :] for z in range(ZL)]
            turned = jnp.concatenate(cells, 0).T.astype(BF)
            target[2 * j] = turned[:64]
            target[2 * j + 1] = turned[64:]

    def mixing(weights):
        @pl.loop(0, 32)
        def _(g):
            at = pl.ds(pl.multiple_of(g * LANES, LANES), LANES)
            re, im = weights[0, :, at].astype(F32), weights[1, :, at].astype(F32)
            re_s, im_s = swap(re), swap(im)
            big_f[pl.ds(2 * g, modes, stride=LANES), :] = jnp.where(lo, re, im_s)
            big_f[pl.ds(2 * g + 1, modes, stride=LANES), :] = jnp.where(lo, re_s, im)
            big_f[pl.ds(64 + 2 * g, modes, stride=LANES), :] = jnp.where(lo, -im, re_s)
            big_f[pl.ds(65 + 2 * g, modes, stride=LANES), :] = jnp.where(lo, -im_s, re)

    to_blocks(state, xs)
    to_blocks(cotangent, cs)
    pl.semaphore_wait(barrier, NP - 1 + NQ - 1)

    send("py", 0, lambda t: xs.at[t], r1, NP)
    own(r1, p, xs[pl.ds(p, 1)])
    own(c1, p, cs[pl.ds(p, 1)])
    mixing(spectral_z)

    @pl.loop(0, modes)
    def _(k):
        mz[k] = big_f[pl.ds(pl.multiple_of(k * LANES, LANES), LANES), :].astype(BF)

    mixing(spectral_y)
    for j in range(2):
        my[j] = big_f[pl.ds(pl.multiple_of((2 * q + j) * LANES, LANES), LANES), :].astype(BF)
    wi2[...] = jnp.zeros_like(wi2)
    wo2[...] = jnp.zeros_like(wo2)
    for j in range(2):
        wi2[j * 64:(j + 1) * 64, j * HID:(j + 1) * HID] = w_in[...]
        wo2[j * 64:(j + 1) * 64, j * HID:(j + 1) * HID] = w_out[...]
    uz[...] = jnp.zeros_like(uz)
    gz[...] = jnp.zeros_like(gz)
    arrived(0, r1, NP)

    def lines(block):
        return block.astype(F32).reshape(rows, LANES)

    def y_analysis(table, field, sends):
        cells_f[...] = lines(field[...])
        for pair in range(ZL // 2):
            two = [cells_f[pl.ds(2 * pair + i, 3 * NP, stride=ZL), :] for i in range(2)]
            both = jnp.concatenate(two, 1).astype(BF)
            spec = dot_nn(table[...], jnp.concatenate([both, both], 0))
            for i in range(2):
                a, b, c, d = (
                    spec[n * modes:(n + 1) * modes, i * LANES:(i + 1) * LANES] for n in range(4)
                )
                spec_f[pl.ds(2 * pair + i, modes, stride=ZL), :] = jnp.where(
                    lo, a + swap(b), swap(c) + d
                )
        sends[...] = spec_f[...].reshape(NQ, 2 * ZL, LANES).astype(BF)

    def y_synthesis(table, spec):
        spec_f[...] = spec[...].astype(F32).reshape(vrows, LANES)
        for pair in range(ZL // 2):
            two = []
            for i in range(2):
                value = spec_f[pl.ds(2 * pair + i, modes, stride=ZL), :]
                other = swap(value)
                two.append(
                    jnp.concatenate(
                        [
                            jnp.where(lo, value, 0.0), jnp.where(lo, 0.0, other),
                            jnp.where(lo, other, 0.0), jnp.where(lo, 0.0, value),
                        ],
                        0,
                    )
                )
            both = jnp.concatenate(two, 1).astype(BF)
            cells = dot_nn(table[...], jnp.concatenate([both, both], 0))
            for i in range(2):
                cells_f[pl.ds(2 * pair + i, 3 * NP, stride=ZL), :] = cells[
                    :, i * LANES:(i + 1) * LANES
                ]

    def z_analysis(high, low, landing, store):
        both = jnp.concatenate([high[...], low[...]], 1)
        for h in range(2):
            block = landing[:, h].astype(F32)
            for j in range(3):
                cells = block[:, j * ZL:(j + 1) * ZL].reshape(NQ * ZL, LANES).astype(BF)
                spec = dot_nn(both, jnp.concatenate([cells, cells], 0))
                re, im = spec[:modes], spec[modes:]
                at = (h * 3 + j) * 2 * modes
                store[pl.ds(at, modes), :] = jnp.where(lo, re, swap(im))
                store[pl.ds(at + modes, modes), :] = jnp.where(lo, swap(re), im)

    def z_synthesis(high, low, source, sends):
        three = jnp.concatenate([high[...], high[...], low[...]], 1)
        for h in range(2):
            out = []
            for j in range(3):
                at = (h * 3 + j) * 2 * modes
                even, odd = source[pl.ds(at, modes), :], source[pl.ds(at + modes, modes), :]
                spec = jnp.concatenate(
                    [jnp.where(lo, even, swap(odd)), jnp.where(lo, swap(even), odd)], 0
                )
                sh, sl = parts_of(spec)
                cells = dot_nn(three, jnp.concatenate([sh, sl, sh], 0))
                out.append(cells.reshape(NQ, ZL, LANES))
            sends[:, h] = jnp.concatenate(out, 1).astype(BF)

    unroll = min(8, modes)

    def z_split(source, sends):
        @pl.loop(0, modes // unroll)
        def _(step):
            for j in range(unroll):
                k = step * unroll + j
                sends[k] = source[pl.ds(k, 16, stride=modes), :].astype(BF)

    def z_mix(source, store, transposed):
        @pl.loop(0, modes // unroll)
        def _(step):
            for j in range(unroll):
                k = step * unroll + j
                high, low = parts_of(source[pl.ds(k, 16, stride=modes), :])
                both = jnp.concatenate([high, low], 0)
                got = dot_nt(both, mz[k]) if transposed else dot_nn(both, mz[k])
                store[pl.ds(k, 16, stride=modes), :] = got[:16] + got[16:]

    def fold(outer):
        top, bottom = outer[:64], swap(outer[64:])
        return top + jnp.where(lo, bottom, -bottom)

    second = (lax.broadcasted_iota(jnp.int32, (vrows, 1), 0) // ZL) % 2 == 1

    def y_mix(landing, dot):
        value = landing[...].reshape(vrows, LANES)
        return jnp.where(second, dot(value, my[1]), dot(value, my[0])).astype(BF).reshape(
            NQ, 2 * ZL, LANES
        )

    send("pz", 1, lambda t: r1.at[pl.ds(2 * t, 2)], z1, NQ)
    own(z1, q, r1[pl.ds(2 * q, 2)].reshape(1, 2, 24, LANES))
    y_analysis(yf, r1, y1s)
    send("pz", 3, lambda t: y1s.at[t], y1, NQ)
    send("py", 2, lambda t: cs.at[t], c1, NP)
    own(y1, q, y1s[pl.ds(q, 1)])
    arrived(1, z1, NQ)
    z_analysis(zfh, zfl, z1, uz)
    z_mix(uz, vz, False)
    z_synthesis(zath, zatl, vz, z2s)
    send("pz", 5, lambda t: z2s.at[t], z2, NQ)
    own(z2, q, z2s[pl.ds(q, 1)])
    arrived(3, y1, NQ)
    y2s[...] = y_mix(y1, dot_nn)
    send("pz", 4, lambda t: y2s.at[t], y2, NQ)
    own(y2, q, y2s[pl.ds(q, 1)])
    z_split(uz, us)
    send("pz", 17, lambda t: us.at[pl.ds(2 * t, 2)], ur, NQ)
    own(ur, q, us[pl.ds(2 * q, 2)].reshape(1, 2, 16, LANES))
    arrived(4, y2, NQ)
    y_synthesis(yat, y2)
    arrived(5, z2, NQ)
    mixb[...] = (cells_f[...].astype(BF).astype(F32) + lines(z2[...])).astype(BF)

    pre[...] = dot_nn(mixb[...], wi2[...])
    arrived(2, c1, NP)
    cot = lines(c1[...]).astype(BF)
    gact[...] = dot_nn(cot, wo2[...])
    tile = 32 if rows % 32 == 0 else 16

    @pl.loop(0, rows // tile)
    def _(step):
        at = pl.ds(pl.multiple_of(step * tile, tile), tile)
        value = pre[at, :]
        root = math.sqrt(2.0 / math.pi)
        square = value * value
        bend = jnp.tanh(value * (root + (root * 0.044715) * square))
        rise = 0.5 + 0.5 * bend
        slope = rise + (0.5 * value) * (1.0 - bend * bend) * (root + (3.0 * root * 0.044715) * square)
        actb[at, :] = (value * rise).astype(BF)
        gpb[at, :] = (gact[at, :] * slope).astype(BF)

    g1[...] = dot_nt(gpb[...], wi2[...]).reshape(NP, 24, LANES).astype(BF)

    send("pz", 6, lambda t: g1.at[pl.ds(2 * t, 2)], z3, NQ)
    own(z3, q, g1[pl.ds(2 * q, 2)].reshape(1, 2, 24, LANES))
    y_analysis(ya, g1, y3s)
    send("pz", 7, lambda t: y3s.at[t], y3, NQ)
    own(y3, q, y3s[pl.ds(q, 1)])

    def diagonal(both):
        return both[:64, :HID] + both[64:, HID:]

    dwi = diagonal(dot_tn(mixb[...], gpb[...]))
    dwo = diagonal(dot_tn(cot, actb[...]))
    m1s[...] = jnp.concatenate(
        [dwi[:, :LANES], dwi[:, LANES:], dwo[:, :LANES], dwo[:, LANES:]], 0
    ).reshape(NP, share, LANES).astype(BF)
    send("py", 8, lambda t: m1s.at[t], m1r, NP)
    own(m1r, p, m1s[pl.ds(p, 1)])

    arrived(6, z3, NQ)
    z_analysis(zah, zal, z3, gz)
    z_split(gz, gs)
    send("pz", 10, lambda t: gs.at[pl.ds(2 * t, 2)], gr, NQ)
    own(gr, q, gs[pl.ds(2 * q, 2)].reshape(1, 2, 16, LANES))
    arrived(7, y3, NQ)
    y4s[...] = y_mix(y3, dot_nt)
    send("pz", 9, lambda t: y4s.at[t], y4, NQ)
    own(y4, q, y4s[pl.ds(q, 1)])

    for landing, store in ((y1, su), (y3, sg)):
        value = landing[...].astype(F32)
        for j in range(2):
            at = value[:, j * ZL:(j + 1) * ZL]
            store[j] = at.reshape(NQ * ZL, LANES).astype(BF)

    @pl.loop(0, 2)
    def _(j):
        dws[j] = fold(dot_tn(su[j], sg[j]))

    def scatter(branch, slot):
        ws[branch] = dws[2 * branch:2 * branch + 2].reshape(half, share, LANES).astype(BF)
        send(branch, slot, lambda t: ws.at[branch, t - branch * half], wr, NP)

        @pl.when(p // half == branch)
        def _():
            own(wr, p, ws[branch, pl.ds(p - branch * half, 1)])

    def gather(branch, slot, into, scale):
        @pl.when(p // half == branch)
        def _():
            arrived(slot, wr, NP)
            wg[...] = (jnp.sum(wr[...].astype(F32), axis=0) * scale).astype(BF)
            own(parts.at[branch], p - branch * half, wg[...].reshape(1, share, LANES))

            @pl.loop(0, half)
            def _(i):
                far = half // 2 + (1 - 2 * lax.rem(i, 2)) * ((i + 1) // 2)
                step = lax.rem(p + far + half, half)
                for side in (0, 1):
                    t = step + lax.rem(branch + 1 + side, 2) * half

                    @pl.when(t != p)
                    def _():
                        pltpu.make_async_remote_copy(
                            src_ref=wg,
                            dst_ref=parts.at[branch, p - branch * half],
                            send_sem=send_sem.at[into],
                            recv_sem=recv_sem.at[into],
                            device_id=(t, q),
                            device_id_type=MESH,
                        ).start()

    def settle(branch, slot, into):
        @pl.when(p // half == branch)
        def _():
            drain(slot, ws.at[branch], half).wait_send()
            drain(into, wr, NP).wait_send()

        @pl.when(p // half != branch)
        def _():
            drain(slot, ws.at[branch], half + 1).wait_send()

    scatter(0, 13)
    z_mix(gz, vz, True)
    z_synthesis(zfth, zftl, vz, z4s)
    send("pz", 11, lambda t: z4s.at[t], z4, NQ)
    own(z4, q, z4s[pl.ds(q, 1)])
    arrived(17, ur, NQ)
    arrived(10, gr, NQ)

    @pl.loop(0, 2)
    def _(j):
        dws[2 + j] = fold(
            dot_tn(ur[:, j].reshape(NQ * 16, LANES), gr[:, j].reshape(NQ * 16, LANES))
        )

    scatter(1, 15)
    arrived(8, m1r, NP)
    own(m2r, q, jnp.sum(m1r[...].astype(F32), axis=0, keepdims=True))
    send("pz", 14, lambda t: m2r.at[q], m2r, NQ)

    arrived(9, y4, NQ)
    y_synthesis(yft, y4)
    arrived(11, z4, NQ)
    total = lines(c1[...]) + cells_f[...].astype(BF).astype(F32) + lines(z4[...])
    o1[...] = total.reshape(NP, 24, LANES).astype(BF)
    scale_y = 1.0 / math.sqrt(NP * ZL * NQ)
    scale_z = 1.0 / math.sqrt(NP * YL * NP)
    scale_mlp = 1.0 / math.sqrt(NP * (YL * NP) * (ZL * NQ))
    gather(0, 13, 16, scale_y)
    send("py", 12, lambda t: o1.at[t], f1, NP, (0, half // 2))
    own(f1, p, o1[pl.ds(p, 1)])
    gather(1, 15, 18, scale_z)
    send("py", 12, lambda t: o1.at[t], f1, NP, (half // 2, half))
    arrived(14, m2r, NQ)
    own(m3r, p, (jnp.sum(m2r[...], axis=0, keepdims=True) * scale_mlp).astype(BF))
    send("py", 19, lambda t: m3r.at[p], m3r, NP)

    def ring(branch, slot, device):
        at = gathered.at[branch, slot]
        return pltpu.make_async_remote_copy(
            src_ref=at,
            dst_ref=at,
            send_sem=send_sem.at[20 + branch],
            recv_sem=ring_sem.at[branch, slot],
            device_id=(p, device),
            device_id_type=MESH,
        )

    def ring_start(branch, into):
        @pl.when(p // half == branch)
        def _():
            drain(into, parts.at[branch], half).wait_recv()

        @pl.when(p // half != branch)
        def _():
            drain(into, parts.at[branch], half + 1).wait_recv()

        own(gathered.at[branch], q, parts[branch].reshape(1, half, share, LANES))

        @pl.loop(1, NQ // 2)
        def _(j):
            ring(branch, q, lax.rem(q + 2 * j, NQ)).start()

        ring(branch, q, sibling).start()

    def ring_pass(branch):
        @pl.loop(1, NQ // 2)
        def _(j):
            slot = lax.rem(q + 2 * j, NQ)
            ring(branch, slot, sibling).wait_recv()
            ring(branch, slot, sibling).start()

    def ring_end(branch, target):
        @pl.loop(0, NQ // 2)
        def _(j):
            ring(branch, lax.rem(sibling + 2 * j, NQ), sibling).wait_recv()

        big_f[:modes * CH, :] = gathered[branch].astype(F32).reshape(modes * CH, LANES)

        @pl.loop(0, 32)
        def _(g):
            at = pl.ds(pl.multiple_of(g * LANES, LANES), LANES)
            even = big_f[pl.ds(2 * g, modes, stride=CH), :]
            odd = big_f[pl.ds(2 * g + 1, modes, stride=CH), :]
            target[0, :, at] = jnp.where(lo, even, swap(odd)).astype(BF)
            target[1, :, at] = jnp.where(lo, swap(even), odd).astype(BF)

    ring_start(0, 16)
    ring_pass(0)
    ring_start(1, 18)
    ring_end(0, grad_sy)
    arrived(12, f1, NP)
    from_blocks(f1, grad_state)
    ring_pass(1)
    arrived(19, m3r, NP)
    small = m3r[...].reshape(256, LANES)
    grad_in[...] = jnp.concatenate([small[:64], small[64:128]], 1)
    grad_out[...] = jnp.concatenate([small[128:192], small[192:]], 1)
    ring_end(1, grad_sz)

    for item in pending:
        drain(*item).wait_send()
    settle(0, 13, 16)
    settle(1, 15, 18)
    for branch in range(2):
        drain(20 + branch, gathered.at[branch], NQ).wait_send()


def on_device(NP, NQ, state, cotangent, spectral_y, spectral_z, w_in, w_out):
    modes = 2 * NQ
    rows = NP * 24
    vrows = modes * ZL
    share = 256 // NP

    forward_y, inverse_y = base_tables(YL * NP, modes)
    forward_z, inverse_z = base_tables(ZL * NQ, modes)
    yf = np_parts(y_tables(forward_y, NP, modes))
    ya = np_parts(y_tables(inverse_y, NP, modes))
    zf = np_parts(np.concatenate(forward_z, 0))
    za = np_parts(np.concatenate(inverse_z, 0))
    tables = [np.concatenate(yf, 1), np.concatenate(ya, 1)]
    tables += [np.concatenate([v.T for v in yf], 1), np.concatenate([v.T for v in ya], 1)]
    tables += [*zf, *za, zf[0].T, zf[1].T, za[0].T, za[1].T]

    vmem = pl.BlockSpec(memory_space=pltpu.VMEM)
    V = pltpu.VMEM
    field = lambda: V((NP, 24, LANES), BF)
    zbuf = lambda: V((NQ, 2, 24, LANES), BF)
    ybuf = lambda: V((NQ, 2 * ZL, LANES), BF)
    pack = lambda kind: V((NP, share, LANES), kind)
    scratch = [
        field(), field(), field(), field(), zbuf(), ybuf(), ybuf(), ybuf(), ybuf(), zbuf(), zbuf(),
        field(), zbuf(), ybuf(), ybuf(), ybuf(), ybuf(), zbuf(), zbuf(), field(), field(),
        V((modes, 16, LANES), BF), V((NQ, 2, 16, LANES), BF),
        V((modes, 16, LANES), BF), V((NQ, 2, 16, LANES), BF),
        V((2, NP // 2, share, LANES), BF), pack(BF), V((share, LANES), BF),
        V((2, NP // 2, share, LANES), BF), V((2, NQ, NP // 2, share, LANES), BF),
        pack(BF), pack(BF), V((NQ, share, LANES), F32), pack(BF),
        V((LANES, 2 * HID), BF), V((LANES, 2 * HID), BF),
        V((2, LANES, LANES), BF), V((modes, LANES, LANES), BF),
        V((rows, 2 * HID), F32), V((rows, 2 * HID), F32),
        V((rows, 2 * HID), BF), V((rows, 2 * HID), BF), V((rows, LANES), BF),
        V((16 * modes, LANES), F32), V((16 * modes, LANES), F32), V((16 * modes, LANES), F32),
        V((2, NQ * ZL, LANES), BF), V((2, NQ * ZL, LANES), BF), V((4, CH, LANES), F32),
        V((rows, LANES), F32), V((vrows, LANES), F32),
        V((ZL * NP, LANES), F32),
        V((max(modes * LANES, rows), LANES), F32),
        pltpu.SemaphoreType.DMA((22,)),
        pltpu.SemaphoreType.DMA((22,)),
        pltpu.SemaphoreType.DMA((2, NQ)),
    ]
    state, cotangent = (jnp.transpose(v, (1, 0, 2)) for v in (state, cotangent))
    shape = lambda like: jax.ShapeDtypeStruct(like.shape, BF)
    grad, grad_sy, grad_sz, grad_in, grad_out = pl.pallas_call(
        functools.partial(kernel, NP, NQ),
        out_shape=tuple(shape(v) for v in (state, spectral_y, spectral_z, w_in, w_in)),
        in_specs=[vmem] * (6 + len(tables)),
        out_specs=(vmem,) * 5,
        scratch_shapes=scratch,
        compiler_params=pltpu.CompilerParams(
            collective_id=0, has_side_effects=True, vmem_limit_bytes=56 * 1024 * 1024
        ),
    )(state, cotangent, spectral_y, spectral_z, w_in, w_out.T, *[jnp.asarray(t) for t in tables])
    return (jnp.transpose(grad, (1, 0, 2)), grad_sy, grad_sz, grad_in, grad_out.T)


def solution(mesh):
    sizes = (mesh.shape["py"], mesh.shape["pz"])
    in_specs = (P(None, "py", "pz"), P(None, "py", "pz"), P(), P(), P(), P())
    out_specs = (P(None, "py", "pz"), P(), P(), P(), P())
    return jax.shard_map(
        functools.partial(on_device, *sizes),
        mesh=mesh,
        in_specs=in_specs,
        out_specs=out_specs,
        check_vma=False,
    )
```

time: 134 us -> 94.3 us (0.70)
  Pallas kernels: 112 us -> 87.6 us
  local copies, waits for them, and re-layouts: 16.6 us -> 5.73 us
  other arithmetic: 4.45 us -> 0 us
    pallas_call x1, Pallas kernels: 112 us -> 87.6 us  [on_device(): pl.pallas_call(functools.partial(kernel, NP, NQ), out_shape=tuple((shape(...]
    squeeze x6 -> x0, local copies, waits for them, and re-layouts: 4.5 us -> none  [the longest x2 3.23 us: on_device(): return (grad_state, spec[0], spec[1], grad_w_in, grad_w_out)]
    reshape x6 -> x0, local copies, waits for them, and re-layouts: 4.42 us -> none  [the longest x2 1.76 us: to_blocks(): return jnp.transpose(cut, (4, 1, 3, 2, 0)).reshape(NP, 24, LANES)]
    slice x6 -> x0, local copies, waits for them, and re-layouts: 3.29 us -> none  [the longest x3 2.28 us: on_device(): return (grad_state, spec[0], spec[1], grad_w_in, grad_w_out)]
    concatenate x2 -> x0, other arithmetic: 2.26 us -> none  [mixing(): jnp.concatenate([jnp.concatenate([re, im], -1), jnp.concatenate([-im, re]...]
    unnamed x11, local copies, waits for them, and re-layouts: 3.56 us -> 5.73 us
where the time goes in v2:
time: 94.3 us; the launch traced here: 94 us
  Pallas kernels  87.6 us (93%)
  local copies, waits for them, and re-layouts  5.73 us (6%)
    pallas_call x1, Pallas kernels, on_device(): pl.pallas_call(functools.partial(kernel, NP, NQ), out_shape=tuple((shape(...  87.6 us
    unnamed x11, local copies, waits for them, and re-layouts  5.73 us

profile of v2, /device:TPU:1, one launch (start us, length us, event | category | flops | bytes accessed | tf_op | source)
XLA Modules:
  0.0 94.0 jit_solution(17951642283891336836)
XLA Ops:
  0.6 87.6 %shard_map.209 = (bf16[6,64,256]{2,1,0:T(8,128)(2,1)}, bf16[2,32,4096]{2,1,0:T(8,128)(2,1)}, bf16[2,32,4096]{2,1,0:T(8,128)(2,1)}, bf16[64,256]{1,0:T(8,128)(2,1)}, bf16[64,256]{1,0:T(8,128)(2,1)}) custom-call(bf16[6,64,256]{2,1,0:T(8,128)(2,1)} %bitcast.5, bf16[6,64,256]{2,1,0:T(8,128)(2,1)} %bitcast.6, bf16[2,32,4096]{2,1,0:T(8,128)(2,1)} %spectral_y.1, ...), custom_call_target="tpu_custom_call" | custom-call | tf_op jit(solution)/shard_map/pallas_call | solution.py:572
  88.3 1.6 %copy.28 = bf16[64,6,256]{2,0,1:T(8,128)(2,1)} copy(bf16[64,6,256]{2,0,1:T(8,128)(2,1)} %bitcast.7) | data formatting | bytes 393216
  89.9 0.0 copy-start
  89.9 1.9 %copy.29 = bf16[2,32,4096]{2,1,0:T(8,128)(2,1)} copy(bf16[2,32,4096]{2,1,0:T(8,128)(2,1)} %get-tuple-element.21) | data formatting | bytes 1048576
  91.8 0.0 copy-done
  91.8 0.0 copy-start.2
  91.8 0.8 copy.30
  92.6 0.0 copy-done.2
  92.6 0.0 copy-start.1
  92.6 0.6 copy.31
  93.2 0.2 copy-done.1
  93.4 0.6 copy.32
Async XLA Ops:
  89.9 1.9 %copy-start = (bf16[2,32,4096]{2,1,0:T(8,128)(2,1)S(1)}, bf16[2,32,4096]{2,1,0:T(8,128)(2,1)}, u32[]{:S(2)}) copy-start(bf16[2,32,4096]{2,1,0:T(8,128)(2,1)} %get-tuple-element.22) | copy-start | bytes 1572868
  91.8 0.8 copy-start.2
  92.6 0.8 copy-start.1

commit v3 on v2

--- a/solution.py
+++ b/solution.py
@@ -59,14 +59,14 @@
 def kernel(
     NP,
     NQ,
-    state, cotangent, spectral_y, spectral_z, w_in, w_out,
-    yf, ya, yft, yat, zfh, zfl, zah, zal, zfth, zftl, zath, zatl,
+    state_in, cot_in, spectral_y, spectral_z, w_in_hbm, w_out_hbm, ytab_hbm, ytabt_hbm, ztab_hbm, ztabt_hbm,
     grad_state, grad_sy, grad_sz, grad_in, grad_out,
     xs, cs, r1, c1, z1, y1s, y1, y2s, y2, z2s, z2, g1, z3, y3s, y3, y4s, y4, z4s, z4, o1, f1,
-    us, ur, gs, gr, ws, wr, wg, parts, gathered, m1s, m1r, m2r, m3r,
-    wi2, wo2, my, mz, pre, gact, actb, gpb, mixb, uz, gz, vz, su, sg, dws,
+    us, ur, gs, gr, ws, wr, wg, parts, m1s, m1r, m2r, m3r,
+    wi2, wo2, my, mz, pre, gact, actb, gpb, mixb, cotb, uz, gz, vz, su, sg, dws,
     cells_f, spec_f, turn_f, big_f,
-    send_sem, recv_sem, ring_sem,
+    weights_f, state, cotangent, w_in, w_out, ytab, ytabt, ztab, ztabt,
+    send_sem, recv_sem, ring_sem, fetch_sem, state_sem,
 ):
     modes = 2 * NQ
     rows = NP * 24
@@ -89,13 +89,13 @@
     lo = lax.broadcasted_iota(jnp.int32, (1, LANES), 1) < 64
     pending = []
 
-    def send(kind, slot, source, landing, n, span=(0, half)):
+    def send(kind, slot, source, landing, n, span=(0, half), each=None):
         def start(t, mine, device):
             pltpu.make_async_remote_copy(
                 src_ref=source(t),
                 dst_ref=landing.at[mine],
                 send_sem=send_sem.at[slot],
-                recv_sem=recv_sem.at[slot],
+                recv_sem=recv_sem.at[slot] if each is None else each.at[mine],
                 device_id=device,
                 device_id_type=MESH,
             ).start()
@@ -159,30 +159,48 @@
             target[2 * j + 1] = turned[64:]
 
     def mixing(weights):
-        @pl.loop(0, 32)
-        def _(g):
-            at = pl.ds(pl.multiple_of(g * LANES, LANES), LANES)
-            re, im = weights[0, :, at].astype(F32), weights[1, :, at].astype(F32)
-            re_s, im_s = swap(re), swap(im)
-            big_f[pl.ds(2 * g, modes, stride=LANES), :] = jnp.where(lo, re, im_s)
-            big_f[pl.ds(2 * g + 1, modes, stride=LANES), :] = jnp.where(lo, re_s, im)
-            big_f[pl.ds(64 + 2 * g, modes, stride=LANES), :] = jnp.where(lo, -im, re_s)
-            big_f[pl.ds(65 + 2 * g, modes, stride=LANES), :] = jnp.where(lo, -im_s, re)
-
+        @pl.loop(0, 8)
+        def _(step):
+            for n in range(4):
+                g = step * 4 + n
+                at = pl.ds(pl.multiple_of(g * LANES, LANES), LANES)
+                re, im = weights[0, :, at].astype(F32), weights[1, :, at].astype(F32)
+                re_s, im_s = swap(re), swap(im)
+                big_f[pl.ds(2 * g, modes, stride=LANES), :] = jnp.where(lo, re, im_s)
+                big_f[pl.ds(2 * g + 1, modes, stride=LANES), :] = jnp.where(lo, re_s, im)
+                big_f[pl.ds(64 + 2 * g, modes, stride=LANES), :] = jnp.where(lo, -im, re_s)
+                big_f[pl.ds(65 + 2 * g, modes, stride=LANES), :] = jnp.where(lo, -im_s, re)
+
+    fetches = [
+        pltpu.make_async_copy(source, target, fetch_sem.at[n])
+        for n, (source, target) in enumerate(
+            [
+                (state_in, state), (cot_in, cotangent),
+                (spectral_z, weights_f.at[0]), (spectral_y, weights_f.at[1]),
+                (w_in_hbm, w_in), (w_out_hbm, w_out),
+                (ytab_hbm, ytab), (ytabt_hbm, ytabt), (ztab_hbm, ztab), (ztabt_hbm, ztabt),
+            ]
+        )
+    ]
+    for fetch in fetches:
+        fetch.start()
+    fetches[0].wait()
     to_blocks(state, xs)
+    pl.semaphore_wait(barrier, NP - 1 + NQ - 1)
+
+    send("py", 0, lambda t: xs.at[t], r1, NP, each=state_sem)
+    own(r1, p, xs[pl.ds(p, 1)])
+    fetches[1].wait()
     to_blocks(cotangent, cs)
-    pl.semaphore_wait(barrier, NP - 1 + NQ - 1)
-
-    send("py", 0, lambda t: xs.at[t], r1, NP)
-    own(r1, p, xs[pl.ds(p, 1)])
-    own(c1, p, cs[pl.ds(p, 1)])
-    mixing(spectral_z)
+    for fetch in fetches[2:]:
+        fetch.wait()
+    mixing(weights_f.at[0])
 
     @pl.loop(0, modes)
     def _(k):
         mz[k] = big_f[pl.ds(pl.multiple_of(k * LANES, LANES), LANES), :].astype(BF)
 
-    mixing(spectral_y)
+    mixing(weights_f.at[1])
     for j in range(2):
         my[j] = big_f[pl.ds(pl.multiple_of((2 * q + j) * LANES, LANES), LANES), :].astype(BF)
     wi2[...] = jnp.zeros_like(wi2)
@@ -192,8 +210,6 @@
         wo2[j * 64:(j + 1) * 64, j * HID:(j + 1) * HID] = w_out[...]
     uz[...] = jnp.zeros_like(uz)
     gz[...] = jnp.zeros_like(gz)
-    arrived(0, r1, NP)
-
     def lines(block):
         return block.astype(F32).reshape(rows, LANES)
 
@@ -235,8 +251,8 @@
                     :, i * LANES:(i + 1) * LANES
                 ]
 
-    def z_analysis(high, low, landing, store):
-        both = jnp.concatenate([high[...], low[...]], 1)
+    def z_analysis(table, landing, store):
+        both = table[...]
         for h in range(2):
             block = landing[:, h].astype(F32)
             for j in range(3):
@@ -247,8 +263,8 @@
                 store[pl.ds(at, modes), :] = jnp.where(lo, re, swap(im))
                 store[pl.ds(at + modes, modes), :] = jnp.where(lo, swap(re), im)
 
-    def z_synthesis(high, low, source, sends):
-        three = jnp.concatenate([high[...], high[...], low[...]], 1)
+    def z_synthesis(table, source, sends):
+        three = table[...]
         for h in range(2):
             out = []
             for j in range(3):
@@ -293,16 +309,51 @@
             NQ, 2 * ZL, LANES
         )
 
-    send("pz", 1, lambda t: r1.at[pl.ds(2 * t, 2)], z1, NQ)
+    quarter = NQ // 2
+
+    @pl.loop(0, quarter)
+    def _(i):
+        far = quarter // 2 + (1 - 2 * lax.rem(i, 2)) * ((i + 1) // 2)
+        step = lax.rem(lax.rem(p, half) // 2 + far + quarter, quarter)
+        for side in (0, 1):
+            t = step + lax.rem(p // half + 1 + side, 2) * quarter
+            for n in range(2):
+                block = 2 * t + n
+
+                @pl.when(block != p)
+                def _():
+                    at = r1.at[block]
+                    pltpu.make_async_remote_copy(
+                        src_ref=at,
+                        dst_ref=at,
+                        send_sem=send_sem.at[0],
+                        recv_sem=state_sem.at[block],
+                        device_id=(p, q),
+                        device_id_type=MESH,
+                    ).wait_recv()
+
+            @pl.when(t != q)
+            def _():
+                pltpu.make_async_remote_copy(
+                    src_ref=r1.at[pl.ds(2 * t, 2)],
+                    dst_ref=z1.at[q],
+                    send_sem=send_sem.at[1],
+                    recv_sem=recv_sem.at[1],
+                    device_id=(p, t),
+                    device_id_type=MESH,
+                ).start()
+
+    pending.append((1, z1, NQ))
     own(z1, q, r1[pl.ds(2 * q, 2)].reshape(1, 2, 24, LANES))
-    y_analysis(yf, r1, y1s)
+    y_analysis(ytab.at[0], r1, y1s)
     send("pz", 3, lambda t: y1s.at[t], y1, NQ)
     send("py", 2, lambda t: cs.at[t], c1, NP)
+    own(c1, p, cs[pl.ds(p, 1)])
     own(y1, q, y1s[pl.ds(q, 1)])
     arrived(1, z1, NQ)
-    z_analysis(zfh, zfl, z1, uz)
+    z_analysis(ztab.at[0], z1, uz)
     z_mix(uz, vz, False)
-    z_synthesis(zath, zatl, vz, z2s)
+    z_synthesis(ztabt.at[1], vz, z2s)
     send("pz", 5, lambda t: z2s.at[t], z2, NQ)
     own(z2, q, z2s[pl.ds(q, 1)])
     arrived(3, y1, NQ)
@@ -313,33 +364,61 @@
     send("pz", 17, lambda t: us.at[pl.ds(2 * t, 2)], ur, NQ)
     own(ur, q, us[pl.ds(2 * q, 2)].reshape(1, 2, 16, LANES))
     arrived(4, y2, NQ)
-    y_synthesis(yat, y2)
+    y_synthesis(ytabt.at[1], y2)
     arrived(5, z2, NQ)
     mixb[...] = (cells_f[...].astype(BF).astype(F32) + lines(z2[...])).astype(BF)
 
-    pre[...] = dot_nn(mixb[...], wi2[...])
     arrived(2, c1, NP)
-    cot = lines(c1[...]).astype(BF)
-    gact[...] = dot_nn(cot, wo2[...])
-    tile = 32 if rows % 32 == 0 else 16
-
-    @pl.loop(0, rows // tile)
-    def _(step):
-        at = pl.ds(pl.multiple_of(step * tile, tile), tile)
-        value = pre[at, :]
-        root = math.sqrt(2.0 / math.pi)
-        square = value * value
-        bend = jnp.tanh(value * (root + (root * 0.044715) * square))
-        rise = 0.5 + 0.5 * bend
-        slope = rise + (0.5 * value) * (1.0 - bend * bend) * (root + (3.0 * root * 0.044715) * square)
-        actb[at, :] = (value * rise).astype(BF)
-        gpb[at, :] = (gact[at, :] * slope).astype(BF)
-
-    g1[...] = dot_nt(gpb[...], wi2[...]).reshape(NP, 24, LANES).astype(BF)
-
-    send("pz", 6, lambda t: g1.at[pl.ds(2 * t, 2)], z3, NQ)
+    cotb[...] = lines(c1[...]).astype(BF)
+    chunks = min(4, NQ)
+    per = rows // chunks
+    tile = 32 if per % 32 == 0 else 16
+    root = math.sqrt(2.0 / math.pi)
+
+    @pl.loop(0, chunks)
+    def _(turn):
+        chunk = lax.rem(turn + 1 + q // (NQ // chunks), chunks)
+        start = pl.multiple_of(chunk * per, per)
+        pre[...] = dot_nn(mixb[pl.ds(start, per), :], wi2[...])
+        gact[...] = dot_nn(cotb[pl.ds(start, per), :], wo2[...])
+
+        @pl.loop(0, per // tile)
+        def _(step):
+            here = pl.ds(pl.multiple_of(step * tile, tile), tile)
+            at = pl.ds(pl.multiple_of(start + step * tile, tile), tile)
+            value = pre[here, :]
+            square = value * value
+            bend = jnp.tanh(value * (root + (root * 0.044715) * square))
+            rise = 0.5 + 0.5 * bend
+            slope = rise + (0.5 * value) * (1.0 - bend * bend) * (
+                root + (3.0 * root * 0.044715) * square
+            )
+            actb[at, :] = (value * rise).astype(BF)
+            gpb[at, :] = (gact[here, :] * slope).astype(BF)
+
+        back = dot_nt(gpb[pl.ds(start, per), :], wi2[...])
+        g1[pl.ds(chunk * (NP // chunks), NP // chunks)] = back.reshape(
+            NP // chunks, 24, LANES
+        ).astype(BF)
+
+        @pl.loop(0, NQ // chunks)
+        def _(n):
+            t = chunk * (NQ // chunks) + n
+
+            @pl.when(t != q)
+            def _():
+                pltpu.make_async_remote_copy(
+                    src_ref=g1.at[pl.ds(2 * t, 2)],
+                    dst_ref=z3.at[q],
+                    send_sem=send_sem.at[6],
+                    recv_sem=recv_sem.at[6],
+                    device_id=(p, t),
+                    device_id_type=MESH,
+                ).start()
+
+    pending.append((6, z3, NQ))
     own(z3, q, g1[pl.ds(2 * q, 2)].reshape(1, 2, 24, LANES))
-    y_analysis(ya, g1, y3s)
+    y_analysis(ytab.at[1], g1, y3s)
     send("pz", 7, lambda t: y3s.at[t], y3, NQ)
     own(y3, q, y3s[pl.ds(q, 1)])
 
@@ -347,7 +426,7 @@
         return both[:64, :HID] + both[64:, HID:]
 
     dwi = diagonal(dot_tn(mixb[...], gpb[...]))
-    dwo = diagonal(dot_tn(cot, actb[...]))
+    dwo = diagonal(dot_tn(cotb[...], actb[...]))
     m1s[...] = jnp.concatenate(
         [dwi[:, :LANES], dwi[:, LANES:], dwo[:, :LANES], dwo[:, LANES:]], 0
     ).reshape(NP, share, LANES).astype(BF)
@@ -355,7 +434,7 @@
     own(m1r, p, m1s[pl.ds(p, 1)])
 
     arrived(6, z3, NQ)
-    z_analysis(zah, zal, z3, gz)
+    z_analysis(ztab.at[1], z3, gz)
     z_split(gz, gs)
     send("pz", 10, lambda t: gs.at[pl.ds(2 * t, 2)], gr, NQ)
     own(gr, q, gs[pl.ds(2 * q, 2)].reshape(1, 2, 16, LANES))
@@ -375,7 +454,12 @@
         dws[j] = fold(dot_tn(su[j], sg[j]))
 
     def scatter(branch, slot):
-        ws[branch] = dws[2 * branch:2 * branch + 2].reshape(half, share, LANES).astype(BF)
+        out = [[], []]
+        for j in range(2):
+            even, odd = (dws[2 * branch + j, pl.ds(n, 32, stride=2), :] for n in range(2))
+            out[0].append(jnp.where(lo, even, swap(odd)))
+            out[1].append(jnp.where(lo, swap(even), odd))
+        ws[branch] = jnp.concatenate(out[0] + out[1], 0).reshape(half, share, LANES).astype(BF)
         send(branch, slot, lambda t: ws.at[branch, t - branch * half], wr, NP)
 
         @pl.when(p // half == branch)
@@ -419,7 +503,7 @@
 
     scatter(0, 13)
     z_mix(gz, vz, True)
-    z_synthesis(zfth, zftl, vz, z4s)
+    z_synthesis(ztabt.at[0], vz, z4s)
     send("pz", 11, lambda t: z4s.at[t], z4, NQ)
     own(z4, q, z4s[pl.ds(q, 1)])
     arrived(17, ur, NQ)
@@ -437,7 +521,7 @@
     send("pz", 14, lambda t: m2r.at[q], m2r, NQ)
 
     arrived(9, y4, NQ)
-    y_synthesis(yft, y4)
+    y_synthesis(ytabt.at[0], y4)
     arrived(11, z4, NQ)
     total = lines(c1[...]) + cells_f[...].astype(BF).astype(F32) + lines(z4[...])
     o1[...] = total.reshape(NP, 24, LANES).astype(BF)
@@ -453,8 +537,10 @@
     own(m3r, p, (jnp.sum(m2r[...], axis=0, keepdims=True) * scale_mlp).astype(BF))
     send("py", 19, lambda t: m3r.at[p], m3r, NP)
 
+    targets = (grad_sy, grad_sz)
+
     def ring(branch, slot, device):
-        at = gathered.at[branch, slot]
+        at = targets[branch].at[:, slot]
         return pltpu.make_async_remote_copy(
             src_ref=at,
             dst_ref=at,
@@ -473,7 +559,8 @@
         def _():
             drain(into, parts.at[branch], half + 1).wait_recv()
 
-        own(gathered.at[branch], q, parts[branch].reshape(1, half, share, LANES))
+        whole = parts[branch].astype(F32).reshape(2, 1, CH, LANES).astype(BF)
+        targets[branch][:, pl.ds(q, 1)] = whole
 
         @pl.loop(1, NQ // 2)
         def _(j):
@@ -488,25 +575,14 @@
             ring(branch, slot, sibling).wait_recv()
             ring(branch, slot, sibling).start()
 
-    def ring_end(branch, target):
+    def ring_end(branch):
         @pl.loop(0, NQ // 2)
         def _(j):
             ring(branch, lax.rem(sibling + 2 * j, NQ), sibling).wait_recv()
 
-        big_f[:modes * CH, :] = gathered[branch].astype(F32).reshape(modes * CH, LANES)
-
-        @pl.loop(0, 32)
-        def _(g):
-            at = pl.ds(pl.multiple_of(g * LANES, LANES), LANES)
-            even = big_f[pl.ds(2 * g, modes, stride=CH), :]
-            odd = big_f[pl.ds(2 * g + 1, modes, stride=CH), :]
-            target[0, :, at] = jnp.where(lo, even, swap(odd)).astype(BF)
-            target[1, :, at] = jnp.where(lo, swap(even), odd).astype(BF)
-
     ring_start(0, 16)
+    ring_start(1, 18)
     ring_pass(0)
-    ring_start(1, 18)
-    ring_end(0, grad_sy)
     arrived(12, f1, NP)
     from_blocks(f1, grad_state)
     ring_pass(1)
@@ -514,14 +590,23 @@
     small = m3r[...].reshape(256, LANES)
     grad_in[...] = jnp.concatenate([small[:64], small[64:128]], 1)
     grad_out[...] = jnp.concatenate([small[128:192], small[192:]], 1)
-    ring_end(1, grad_sz)
+    ring_end(0)
+    ring_end(1)
 
     for item in pending:
         drain(*item).wait_send()
     settle(0, 13, 16)
     settle(1, 15, 18)
     for branch in range(2):
-        drain(20 + branch, gathered.at[branch], NQ).wait_send()
+        span = targets[branch].at[:, pl.ds(0, NQ - 1)]
+        pltpu.make_async_remote_copy(
+            src_ref=span,
+            dst_ref=span,
+            send_sem=send_sem.at[20 + branch],
+            recv_sem=ring_sem.at[branch, 0],
+            device_id=(p, q),
+            device_id_type=MESH,
+        ).wait_send()
 
 
 def on_device(NP, NQ, state, cotangent, spectral_y, spectral_z, w_in, w_out):
@@ -536,9 +621,13 @@
     ya = np_parts(y_tables(inverse_y, NP, modes))
     zf = np_parts(np.concatenate(forward_z, 0))
     za = np_parts(np.concatenate(inverse_z, 0))
-    tables = [np.concatenate(yf, 1), np.concatenate(ya, 1)]
-    tables += [np.concatenate([v.T for v in yf], 1), np.concatenate([v.T for v in ya], 1)]
-    tables += [*zf, *za, zf[0].T, zf[1].T, za[0].T, za[1].T]
+    flip = lambda pair: [v.T for v in pair]
+    tables = [
+        np.stack([np.concatenate(v, 1) for v in (yf, ya)]),
+        np.stack([np.concatenate(flip(v), 1) for v in (yf, ya)]),
+        np.stack([np.concatenate(v, 1) for v in (zf, za)]),
+        np.stack([np.concatenate([v[0].T, v[0].T, v[1].T], 1) for v in (zf, za)]),
+    ]
 
     vmem = pl.BlockSpec(memory_space=pltpu.VMEM)
     V = pltpu.VMEM
@@ -552,33 +641,40 @@
         V((modes, 16, LANES), BF), V((NQ, 2, 16, LANES), BF),
         V((modes, 16, LANES), BF), V((NQ, 2, 16, LANES), BF),
         V((2, NP // 2, share, LANES), BF), pack(BF), V((share, LANES), BF),
-        V((2, NP // 2, share, LANES), BF), V((2, NQ, NP // 2, share, LANES), BF),
+        V((2, NP // 2, share, LANES), BF),
         pack(BF), pack(BF), V((NQ, share, LANES), F32), pack(BF),
         V((LANES, 2 * HID), BF), V((LANES, 2 * HID), BF),
         V((2, LANES, LANES), BF), V((modes, LANES, LANES), BF),
-        V((rows, 2 * HID), F32), V((rows, 2 * HID), F32),
-        V((rows, 2 * HID), BF), V((rows, 2 * HID), BF), V((rows, LANES), BF),
+        V((rows // min(4, NQ), 2 * HID), F32), V((rows // min(4, NQ), 2 * HID), F32),
+        V((rows, 2 * HID), BF), V((rows, 2 * HID), BF), V((rows, LANES), BF), V((rows, LANES), BF),
         V((16 * modes, LANES), F32), V((16 * modes, LANES), F32), V((16 * modes, LANES), F32),
         V((2, NQ * ZL, LANES), BF), V((2, NQ * ZL, LANES), BF), V((4, CH, LANES), F32),
         V((rows, LANES), F32), V((vrows, LANES), F32),
         V((ZL * NP, LANES), F32),
         V((max(modes * LANES, rows), LANES), F32),
+        V((2, 2, modes, CH * CH), BF),
+        V((YL, CH, ZL * NP), BF), V((YL, CH, ZL * NP), BF), V((CH, HID), BF), V((CH, HID), BF),
+        *[V(t.shape, BF) for t in tables],
         pltpu.SemaphoreType.DMA((22,)),
         pltpu.SemaphoreType.DMA((22,)),
         pltpu.SemaphoreType.DMA((2, NQ)),
+        pltpu.SemaphoreType.DMA((10,)),
+        pltpu.SemaphoreType.DMA((NP,)),
     ]
     state, cotangent = (jnp.transpose(v, (1, 0, 2)) for v in (state, cotangent))
-    shape = lambda like: jax.ShapeDtypeStruct(like.shape, BF)
+    shape = lambda like: V(like.shape, BF)
+    spec = V((2, NQ, CH, LANES), BF)
     grad, grad_sy, grad_sz, grad_in, grad_out = pl.pallas_call(
         functools.partial(kernel, NP, NQ),
-        out_shape=tuple(shape(v) for v in (state, spectral_y, spectral_z, w_in, w_in)),
-        in_specs=[vmem] * (6 + len(tables)),
+        out_shape=(shape(state), spec, spec, shape(w_in), shape(w_in)),
+        in_specs=[pl.BlockSpec(memory_space=pl.ANY)] * (6 + len(tables)),
         out_specs=(vmem,) * 5,
         scratch_shapes=scratch,
         compiler_params=pltpu.CompilerParams(
             collective_id=0, has_side_effects=True, vmem_limit_bytes=56 * 1024 * 1024
         ),
     )(state, cotangent, spectral_y, spectral_z, w_in, w_out.T, *[jnp.asarray(t) for t in tables])
+    grad_sy, grad_sz = (v.reshape(2, modes, CH * CH) for v in (grad_sy, grad_sz))
     return (jnp.transpose(grad, (1, 0, 2)), grad_sy, grad_sz, grad_in, grad_out.T)
 
 

time: 94.3 us -> 86.8 us (0.920)
  Pallas kernels: 87.6 us -> 82 us
  local copies, waits for them, and re-layouts: 5.73 us -> 3.94 us
    pallas_call x1, Pallas kernels: 87.6 us -> 82 us  [on_device(): pl.pallas_call(functools.partial(kernel, NP, NQ), out_shape=(shape(state)...]
    unnamed x11 -> x3, local copies, waits for them, and re-layouts: 5.73 us -> 1.91 us
    reshape x0 -> x2, local copies, waits for them, and re-layouts: none -> 2.03 us  [on_device(): v.reshape(2, modes, CH * CH)]
where the time goes in v3:
time: 86.8 us; the launch traced here: 86.6 us
  Pallas kernels  82 us (94%)
  local copies, waits for them, and re-layouts  3.94 us (5%)
    pallas_call x1, Pallas kernels, on_device(): pl.pallas_call(functools.partial(kernel, NP, NQ), out_shape=(shape(state)...  82 us
    reshape x2, local copies, waits for them, and re-layouts, on_device(): v.reshape(2, modes, CH * CH)  2.03 us
    unnamed x3, local copies, waits for them, and re-layouts  1.91 us

profile of v3, /device:TPU:1, one launch (start us, length us, event | category | flops | bytes accessed | tf_op | source)
XLA Modules:
  0.0 86.6 jit_solution(1205609679382331248)
XLA Ops:
  0.6 82.0 %shard_map.137 = (bf16[6,64,256]{2,1,0:T(8,128)(2,1)S(1)}, bf16[2,16,64,128]{3,2,1,0:T(8,128)(2,1)S(1)}, bf16[2,16,64,128]{3,2,1,0:T(8,128)(2,1)S(1)}, bf16[64,256]{1,0:T(8,128)(2,1)S(1)}, bf16[64,256]{1,0:T(8,128)(2,1)S(1)}) custom-call(bf16[6,64,256]{2,1,0:T(8,128)(2,1)} %bitcast.11, bf16[6,64,256]{2,1,0:T(8,128)(2,1)} %bitcast.12, ...), custom_call_target="tpu_custom_call" | custom-call | tf_op jit(solution)/shard_map/pallas_call | solution.py:667
  82.7 0.7 copy.18
  83.4 0.6 copy.19
  84.0 0.6 copy.20
  84.6 1.0 %reshape.16 = bf16[2,32,4096]{2,1,0:T(8,128)(2,1)} reshape(bf16[2,16,64,128]{3,2,1,0:T(8,128)(2,1)S(1)} %get-tuple-element.11) | data formatting | bytes 1048576 | tf_op jit(solution)/shard_map/reshape | solution.py:677
  85.6 1.0 %reshape.17 = bf16[2,32,4096]{2,1,0:T(8,128)(2,1)} reshape(bf16[2,16,64,128]{3,2,1,0:T(8,128)(2,1)S(1)} %get-tuple-element.12) | data formatting | bytes 1048576 | tf_op jit(solution)/shard_map/reshape | solution.py:677

commit v4 on v3

--- a/solution.py
+++ b/solution.py
@@ -529,10 +529,10 @@
     scale_z = 1.0 / math.sqrt(NP * YL * NP)
     scale_mlp = 1.0 / math.sqrt(NP * (YL * NP) * (ZL * NQ))
     gather(0, 13, 16, scale_y)
-    send("py", 12, lambda t: o1.at[t], f1, NP, (0, half // 2))
+    send("py", 12, lambda t: o1.at[t], f1, NP, (0, half // 4))
     own(f1, p, o1[pl.ds(p, 1)])
     gather(1, 15, 18, scale_z)
-    send("py", 12, lambda t: o1.at[t], f1, NP, (half // 2, half))
+    send("py", 12, lambda t: o1.at[t], f1, NP, (half // 4, half))
     arrived(14, m2r, NQ)
     own(m3r, p, (jnp.sum(m2r[...], axis=0, keepdims=True) * scale_mlp).astype(BF))
     send("py", 19, lambda t: m3r.at[p], m3r, NP)
@@ -583,9 +583,9 @@
     ring_start(0, 16)
     ring_start(1, 18)
     ring_pass(0)
+    ring_pass(1)
     arrived(12, f1, NP)
     from_blocks(f1, grad_state)
-    ring_pass(1)
     arrived(19, m3r, NP)
     small = m3r[...].reshape(256, LANES)
     grad_in[...] = jnp.concatenate([small[:64], small[64:128]], 1)

time: 86.8 us -> 84.2 us (0.970)
  Pallas kernels: 82 us -> 79.5 us
    pallas_call x1, Pallas kernels: 82 us -> 79.5 us  [on_device(): pl.pallas_call(functools.partial(kernel, NP, NQ), out_shape=(shape(state)...]
where the time goes in v4:
time: 84.2 us; the launch traced here: 84 us
  Pallas kernels  79.5 us (94%)
  local copies, waits for them, and re-layouts  3.94 us (5%)
    pallas_call x1, Pallas kernels, on_device(): pl.pallas_call(functools.partial(kernel, NP, NQ), out_shape=(shape(state)...  79.5 us
    reshape x2, local copies, waits for them, and re-layouts, on_device(): v.reshape(2, modes, CH * CH)  2.03 us
    unnamed x3, local copies, waits for them, and re-layouts  1.91 us

profile of v4, /device:TPU:1, one launch (start us, length us, event | category | flops | bytes accessed | tf_op | source)
XLA Modules:
  0.0 84.0 jit_solution(9920536640667229339)
XLA Ops:
  0.6 79.5 %shard_map.137 = (bf16[6,64,256]{2,1,0:T(8,128)(2,1)S(1)}, bf16[2,16,64,128]{3,2,1,0:T(8,128)(2,1)S(1)}, bf16[2,16,64,128]{3,2,1,0:T(8,128)(2,1)S(1)}, bf16[64,256]{1,0:T(8,128)(2,1)S(1)}, bf16[64,256]{1,0:T(8,128)(2,1)S(1)}) custom-call(bf16[6,64,256]{2,1,0:T(8,128)(2,1)} %bitcast.11, bf16[6,64,256]{2,1,0:T(8,128)(2,1)} %bitcast.12, ...), custom_call_target="tpu_custom_call" | custom-call | tf_op jit(solution)/shard_map/pallas_call | solution.py:667
  80.1 0.7 copy.18
  80.8 0.6 copy.19
  81.4 0.6 copy.20
  82.0 1.0 %reshape.16 = bf16[2,32,4096]{2,1,0:T(8,128)(2,1)} reshape(bf16[2,16,64,128]{3,2,1,0:T(8,128)(2,1)S(1)} %get-tuple-element.11) | data formatting | bytes 1048576 | tf_op jit(solution)/shard_map/reshape | solution.py:677
  83.0 1.0 %reshape.17 = bf16[2,32,4096]{2,1,0:T(8,128)(2,1)} reshape(bf16[2,16,64,128]{3,2,1,0:T(8,128)(2,1)S(1)} %get-tuple-element.12) | data formatting | bytes 1048576 | tf_op jit(solution)/shard_map/reshape | solution.py:677

commit v5 on v4

--- a/solution.py
+++ b/solution.py
@@ -78,9 +78,19 @@
 
     barrier = pltpu.get_barrier_semaphore()
 
-    @pl.loop(1, NP)
+    first = pltpu.make_async_copy(state_in, state, fetch_sem.at[0])
+    first.start()
+
+    @pl.loop(0, half)
     def _(i):
-        pl.semaphore_signal(barrier, inc=1, device_id=(lax.rem(p + i, NP), q), device_id_type=MESH)
+        far = half // 2 + (1 - 2 * lax.rem(i, 2)) * ((i + 1) // 2)
+        step = lax.rem(p + far + half, half)
+        for side in (1, 0):
+            t = step + lax.rem(p // half + side, 2) * half
+
+            @pl.when(t != p)
+            def _():
+                pl.semaphore_signal(barrier, inc=1, device_id=(t, q), device_id_type=MESH)
 
     @pl.loop(1, NQ)
     def _(i):
@@ -182,9 +192,9 @@
             ]
         )
     ]
-    for fetch in fetches:
+    for fetch in fetches[1:]:
         fetch.start()
-    fetches[0].wait()
+    first.wait()
     to_blocks(state, xs)
     pl.semaphore_wait(barrier, NP - 1 + NQ - 1)
 

time: 84.2 us -> 84.3 us (level)
  no operation moved by 1% of the time
where the time goes in v5:
time: 84.3 us; the launch traced here: 84.1 us
  Pallas kernels  79.6 us (94%)
  local copies, waits for them, and re-layouts  3.94 us (5%)
    pallas_call x1, Pallas kernels, on_device(): pl.pallas_call(functools.partial(kernel, NP, NQ), out_shape=(shape(state)...  79.6 us
    reshape x2, local copies, waits for them, and re-layouts, on_device(): v.reshape(2, modes, CH * CH)  2.03 us
    unnamed x3, local copies, waits for them, and re-layouts  1.91 us

profile of v5, /device:TPU:1, one launch (start us, length us, event | category | flops | bytes accessed | tf_op | source)
XLA Modules:
  0.0 84.1 jit_solution(9180463206529557404)
XLA Ops:
  0.6 79.6 %shard_map.137 = (bf16[6,64,256]{2,1,0:T(8,128)(2,1)S(1)}, bf16[2,16,64,128]{3,2,1,0:T(8,128)(2,1)S(1)}, bf16[2,16,64,128]{3,2,1,0:T(8,128)(2,1)S(1)}, bf16[64,256]{1,0:T(8,128)(2,1)S(1)}, bf16[64,256]{1,0:T(8,128)(2,1)S(1)}) custom-call(bf16[6,64,256]{2,1,0:T(8,128)(2,1)} %bitcast.11, bf16[6,64,256]{2,1,0:T(8,128)(2,1)} %bitcast.12, ...), custom_call_target="tpu_custom_call" | custom-call | tf_op jit(solution)/shard_map/pallas_call | solution.py:677
  80.2 0.7 copy.18
  80.9 0.6 copy.19
  81.5 0.6 copy.20
  82.1 1.0 %reshape.16 = bf16[2,32,4096]{2,1,0:T(8,128)(2,1)} reshape(bf16[2,16,64,128]{3,2,1,0:T(8,128)(2,1)S(1)} %get-tuple-element.11) | data formatting | bytes 1048576 | tf_op jit(solution)/shard_map/reshape | solution.py:687
  83.1 1.0 %reshape.17 = bf16[2,32,4096]{2,1,0:T(8,128)(2,1)} reshape(bf16[2,16,64,128]{3,2,1,0:T(8,128)(2,1)S(1)} %get-tuple-element.12) | data formatting | bytes 1048576 | tf_op jit(solution)/shard_map/reshape | solution.py:687
